TPU v7x, 32 devices: a whole 2x2x4 slice. The times are simulated.
32 devices in a mesh: dp: 16 (over z, y, core), tensor: 2 (over x).
Axes of the slice: x: 2, y: 2, z: 4, core: 2. Of those that a mesh axis runs over, the one named last changes fastest.
Arguments:
- tokens: bfloat16 [32768, 1024], P('dp'), may hold values from -6 to 6
- cotangent: bfloat16 [32768, 1024], P('dp'), may hold values from -6 to 6
- lengths: int32 [16, 3], P('dp'), may hold values from 1 to 1228, 2048 in all within a row
- mixer_gain: bfloat16 [1024], replicated, may hold values from 0.5 to 1.5
- in_weight: bfloat16 [1024, 3, 1024], P(None, None, 'tensor'), may hold values from -0.1875 to 0.1875
- conv_weight: bfloat16 [3, 1024], P(None, 'tensor'), may hold values from -3.5 to 3.5
- out_weight: bfloat16 [1024, 1024], P('tensor'), may hold values from -0.1875 to 0.1875
- ffn_gain: bfloat16 [1024], replicated, may hold values from 0.5 to 1.5
- gate_weight: bfloat16 [1024, 4608], P(None, 'tensor'), may hold values from -0.1875 to 0.1875
- up_weight: bfloat16 [1024, 4608], P(None, 'tensor'), may hold values from -0.1875 to 0.1875
- down_weight: bfloat16 [4608, 1024], P('tensor'), may hold values from -0.09375 to 0.09375
Outputs:
- output: bfloat16 [32768, 1024], P('dp')
- input_grad: bfloat16 [32768, 1024], P('dp')
- mixer_gain_grad: float32 [1024], replicated
- in_weight_grad: float32 [1024, 3, 1024], P(None, None, 'tensor')
- conv_weight_grad: float32 [3, 1024], P(None, 'tensor')
- out_weight_grad: float32 [1024, 1024], P('tensor')
- ffn_gain_grad: float32 [1024], replicated
- gate_weight_grad: float32 [1024, 4608], P(None, 'tensor')
- up_weight_grad: float32 [1024, 4608], P(None, 'tensor')
- down_weight_grad: float32 [4608, 1024], P('tensor')
Inputs may be any that keep to these rules, and one draw needn't show every extreme that they name: `lengths`: each row sums to 2048, and its largest entry is exactly 1228.
All inputs are finite; a program needn't handle non-finite values.
Results may differ from a plain program's by a relative error of at most 0.011.
Values may be sent and summed in bfloat16 or wider, within the bound.
A program may use at most 320 MiB of HBM per device.

v0:
```python
import jax
import jax.numpy as jnp
from jax import lax
from jax.sharding import PartitionSpec as P

EPS = 1e-05


def distances(lengths, count):
    ends = jnp.cumsum(lengths)
    starts = ends - lengths
    places = jnp.arange(count, dtype=jnp.int32)
    begin = jnp.max(jnp.where(starts[None, :] <= places[:, None], starts[None, :], 0), axis=1)
    return places - begin


def rms_scale(value):
    return lax.rsqrt(jnp.mean(value * value, axis=-1, keepdims=True) + EPS)


def shift_down(value, steps, keep):
    moved = jnp.concatenate([jnp.zeros_like(value[:steps]), value[:-steps]], 0)
    return moved * keep


def shift_up(value, steps):
    return jnp.concatenate([value[steps:], jnp.zeros_like(value[:steps])], 0)


def norm_back(grad_in, normed, scale, gain):
    weighted = grad_in * gain
    inner = jnp.mean(weighted * normed, axis=-1, keepdims=True)
    return (scale * (weighted - normed * inner), jnp.sum(grad_in * normed, axis=0))


def body(
    tokens,
    cotangent,
    lengths,
    mixer_gain,
    in_weight,
    conv_weight,
    out_weight,
    ffn_gain,
    gate_weight,
    up_weight,
    down_weight,
):
    rows = tokens.shape[0]
    dist = distances(lengths[0], rows)
    keep_one = (dist >= 1)[:, None].astype(jnp.float32)
    keep_two = (dist >= 2)[:, None].astype(jnp.float32)
    parts = lax.axis_size("tensor")
    share = rows // parts
    first = lax.axis_index("tensor") * share
    x = tokens.astype(jnp.float32)
    dy = cotangent.astype(jnp.float32)
    g1 = mixer_gain.astype(jnp.float32)
    g2 = ffn_gain.astype(jnp.float32)
    taps = conv_weight.astype(jnp.float32)
    scale1 = rms_scale(x)
    normed1 = x * scale1
    h1b = (normed1 * g1).astype(jnp.bfloat16)
    proj = jnp.einsum("td,dkc->tkc", h1b, in_weight, preferred_element_type=jnp.float32)
    b_part, c_part, x_part = (proj[:, 0], proj[:, 1], proj[:, 2])
    mixed = b_part * x_part
    mixed_one = shift_down(mixed, 1, keep_one)
    mixed_two = shift_down(mixed, 2, keep_two)
    conv_out = taps[0] * mixed + taps[1] * mixed_one + taps[2] * mixed_two
    zb = (c_part * conv_out).astype(jnp.bfloat16)
    mix_part = jnp.dot(zb, out_weight, preferred_element_type=jnp.float32)
    mix_rows = lax.psum_scatter(mix_part, "tensor", scatter_dimension=0, tiled=True)
    x_rows = lax.dynamic_slice_in_dim(x, first, share, 0)
    resid = x_rows + mix_rows
    scale2 = rms_scale(resid)
    normed2 = resid * scale2
    h2b = lax.all_gather((normed2 * g2).astype(jnp.bfloat16), "tensor", axis=0, tiled=True)
    gate = jnp.dot(h2b, gate_weight, preferred_element_type=jnp.float32)
    up = jnp.dot(h2b, up_weight, preferred_element_type=jnp.float32)
    sig = jax.nn.sigmoid(gate)
    silu = gate * sig
    hidb = (silu * up).astype(jnp.bfloat16)
    ffn_part = jnp.dot(hidb, down_weight, preferred_element_type=jnp.float32)
    down_grad = jnp.einsum("tf,td->fd", hidb, cotangent, preferred_element_type=jnp.float32)
    d_hid = jnp.einsum("td,fd->tf", cotangent, down_weight, preferred_element_type=jnp.float32)
    d_gate = (d_hid * up * sig * (1.0 + gate * (1.0 - sig))).astype(jnp.bfloat16)
    d_up = (d_hid * silu).astype(jnp.bfloat16)
    gate_grad = jnp.einsum("td,tf->df", h2b, d_gate, preferred_element_type=jnp.float32)
    up_grad = jnp.einsum("td,tf->df", h2b, d_up, preferred_element_type=jnp.float32)
    dh2_part = jnp.einsum("tf,df->td", d_gate, gate_weight, preferred_element_type=jnp.float32)
    dh2_part = dh2_part + jnp.einsum(
        "tf,df->td", d_up, up_weight, preferred_element_type=jnp.float32
    )
    ffn_rows = lax.psum_scatter(
        ffn_part.astype(jnp.bfloat16), "tensor", scatter_dimension=0, tiled=True
    ).astype(jnp.float32)
    output = lax.all_gather((resid + ffn_rows).astype(jnp.bfloat16), "tensor", axis=0, tiled=True)
    dh2_rows = lax.psum_scatter(dh2_part, "tensor", scatter_dimension=0, tiled=True)
    d_resid, g2_grad = norm_back(dh2_rows, normed2, scale2, g2)
    dr1 = lax.dynamic_slice_in_dim(dy, first, share, 0) + d_resid
    dr1b = lax.all_gather(dr1.astype(jnp.bfloat16), "tensor", axis=0, tiled=True)
    out_grad = jnp.einsum("tc,td->cd", zb, dr1b, preferred_element_type=jnp.float32)
    d_z = jnp.einsum("td,cd->tc", dr1b, out_weight, preferred_element_type=jnp.float32)
    d_c = d_z * conv_out
    d_conv = d_z * c_part
    conv_grad = jnp.stack(
        [
            jnp.sum(d_conv * mixed, axis=0),
            jnp.sum(d_conv * mixed_one, axis=0),
            jnp.sum(d_conv * mixed_two, axis=0),
        ],
        0,
    )
    d_mixed = (
        taps[0] * d_conv
        + taps[1] * shift_up(d_conv * keep_one, 1)
        + taps[2] * shift_up(d_conv * keep_two, 2)
    )
    d_proj = jnp.stack([d_mixed * x_part, d_c, d_mixed * b_part], 1).astype(jnp.bfloat16)
    in_grad_w = jnp.einsum("td,tkc->dkc", h1b, d_proj, preferred_element_type=jnp.float32)
    dh1_part = jnp.einsum("tkc,dkc->td", d_proj, in_weight, preferred_element_type=jnp.float32)
    dh1_rows = lax.psum_scatter(dh1_part, "tensor", scatter_dimension=0, tiled=True)
    normed1_rows = lax.dynamic_slice_in_dim(normed1, first, share, 0)
    scale1_rows = lax.dynamic_slice_in_dim(scale1, first, share, 0)
    d_input, g1_grad = norm_back(dh1_rows, normed1_rows, scale1_rows, g1)
    input_grad = lax.all_gather((dr1 + d_input).astype(jnp.bfloat16), "tensor", axis=0, tiled=True)
    g1_grad, g2_grad = lax.psum((g1_grad, g2_grad), "tensor")
    summed = lax.psum(
        (g1_grad, in_grad_w, conv_grad, out_grad, g2_grad, gate_grad, up_grad, down_grad), "dp"
    )
    return (
        output,
        input_grad,
        summed[0],
        summed[1],
        summed[2],
        summed[3],
        summed[4],
        summed[5],
        summed[6],
        summed[7],
    )


def solution(mesh):
    return jax.shard_map(
        body,
        mesh=mesh,
        in_specs=(
            P("dp", None),
            P("dp", None),
            P("dp", None),
            P(),
            P(None, None, "tensor"),
            P(None, "tensor"),
            P("tensor", None),
            P(),
            P(None, "tensor"),
            P(None, "tensor"),
            P("tensor", None),
        ),
        out_specs=(
            P("dp", None),
            P("dp", None),
            P(),
            P(None, None, "tensor"),
            P(None, "tensor"),
            P("tensor", None),
            P(),
            P(None, "tensor"),
            P(None, "tensor"),
            P("tensor", None),
        ),
        check_vma=False,
    )
```

profile of v0, /device:TPU:0, one launch (start us, length us, event | category | flops | bytes accessed | tf_op | source)
XLA Modules:
  0.0 1458.4 jit_solution(14518880325677875519)
XLA Ops:
  7.2 0.8 convert_element_type.66
  8.1 3.5 multiply_reduce_fusion
  11.6 6.9 fusion.9
  18.6 4.5 copy-done.3
  23.1 3.0 fusion.3
  26.1 0.2 reduce-window_clone.1
  26.3 0.1 select_reduce_fusion
  26.5 10.7 multiply_convert_fusion.8
  37.2 1.3 copy-done.16
  38.5 5.9 fusion.16
  44.4 0.3 all-gather.5.cloned.1.call-start
  44.7 6.6 convert_element_type.65
  51.3 95.2 %reduce-scatter.5.cloned.1.call-done = f32[1024,1024]{1,0:T(8,128)} async-done(((f32[2048,1024]{1,0:T(8,128)}), f32[1024,1024]{1,0:T(8,128)}) %reduce-scatter.5.cloned.1.call-update) | async-done | bytes 4194320 | tf_op jit(solution)/shard_map/reduce_scatter | solution.py:72
  146.5 4.0 multiply_reduce_fusion.8
  150.5 2.0 copy-done.1
  152.5 1.7 multiply_convert_fusion.7
  154.3 56.9 %all-gather.5.cloned.1.call-done = bf16[2048,1024]{1,0:T(8,128)(2,1)} async-done(((bf16[1024,1024]{1,0:T(8,128)(2,1)}), bf16[2048,1024]{1,0:T(8,128)(2,1)}) %all-gather.5.cloned.1.call-update) | async-done | bytes 4194320 | tf_op jit(solution)/shard_map/all_gather | solution.py:77
  211.2 16.9 %fusion.17 = f32[2048,2304]{1,0:T(8,128)} fusion(bf16[2048,1024]{1,0:T(8,128)(2,1)} %all-gather.5.cloned.1.call-done, bf16[1024,2304]{1,0:T(8,128)(2,1)} %param.19), kind=kOutput, calls=%fused_computation.62 | convolution fusion | flops 9663676416 | bytes 27787264 | tf_op jit(solution)/shard_map/dot_general | solution.py:78
  228.0 15.4 %fusion.18 = f32[2048,2304]{1,0:T(8,128)} fusion(bf16[2048,1024]{1,0:T(8,128)(2,1)S(1)} %copy-done.36, bf16[1024,2304]{1,0:T(8,128)(2,1)} %param.20), kind=kOutput, calls=%fused_computation.63 | convolution fusion | flops 9663676416 | bytes 27787264 | tf_op jit(solution)/shard_map/dot_general | solution.py:79
  243.4 35.6 %multiply_convert_fusion = (bf16[2048,2304]{1,0:T(8,128)(2,1)}, bf16[2048,2304]{1,0:T(8,128)(2,1)}, bf16[2048,2304]{1,0:T(8,128)(2,1)}) fusion(f32[2048,2304]{1,0:T(8,128)} %fusion.17, f32[2048,2304]{1,0:T(8,128)} %fusion.18, bf16[2048,1024]{1,0:T(8,128)(2,1)} %param.12, bf16[2304,1024]{1,0:T(8,128)(2,1)} %param.21), kind=kOutput, calls=%fused_computation | convolution fusion | flops 9734455296 | bytes 74973184 | tf_op jit(solution)/shard_map/td,fd->tf/dot_general | solution.py:85
  279.0 16.1 %fusion.19 = f32[2048,1024]{1,0:T(8,128)} fusion(bf16[2048,2304]{1,0:T(8,128)(2,1)} %get-tuple-element.35, bf16[1024,2304]{1,0:T(8,128)(2,1)} %param.19), kind=kOutput, calls=%fused_computation.64 | convolution fusion | flops 9663676416 | bytes 22544384 | tf_op jit(solution)/shard_map/tf,df->td/dot_general | solution.py:90
  295.1 15.7 %convolution_add_fusion = f32[2048,1024]{1,0:T(8,128)} fusion(f32[2048,1024]{1,0:T(8,128)} %fusion.19, bf16[2048,2304]{1,0:T(8,128)(2,1)S(1)} %copy-done.39, bf16[1024,2304]{1,0:T(8,128)(2,1)} %param.20), kind=kOutput, calls=%fused_computation.39 | convolution fusion | flops 9665773568 | bytes 30932992 | tf_op jit(solution)/shard_map/tf,df->td/dot_general | solution.py:91
  310.9 99.3 %reduce-scatter.9.cloned.1.call-done = f32[1024,1024]{1,0:T(8,128)} async-done(((f32[2048,1024]{1,0:T(8,128)}), f32[1024,1024]{1,0:T(8,128)}) %reduce-scatter.9.cloned.1.call-update) | async-done | bytes 4194320 | tf_op jit(solution)/shard_map/reduce_scatter | solution.py:98
  410.2 4.7 multiply_reduce_fusion.1
  414.9 1.2 copy-done.6
  416.1 3.6 fusion.13
  419.9 0.1 slice.54
  419.9 0.1 slice.52
  420.0 56.7 %all-gather.9.cloned.1.call-done = bf16[2048,1024]{1,0:T(8,128)(2,1)} async-done(((bf16[1024,1024]{1,0:T(8,128)(2,1)}), bf16[2048,1024]{1,0:T(8,128)(2,1)}) %all-gather.9.cloned.1.call-update) | async-done | bytes 4194320 | tf_op jit(solution)/shard_map/all_gather | solution.py:101
  476.7 13.3 multiply_reduce_fusion.4
  490.0 0.5 slice_multiply_fusion
  490.6 0.5 slice_multiply_fusion.1
  491.1 1.1 slice-done.2
  492.2 3.3 fusion.5
  495.5 1.2 fusion.7
  496.7 1.3 copy-done.13
  498.0 8.8 convolution_bitcast_fusion
  506.9 15.2 %convolution_convert_fusion = bf16[2048,1024]{1,0:T(8,128)(2,1)} fusion(bf16[2048,2304]{1,0:T(8,128)(2,1)} %get-tuple-element.36, bf16[2304,1024]{1,0:T(8,128)(2,1)} %param.21), kind=kOutput, calls=%fused_computation.40 | convolution fusion | flops 9665773568 | bytes 18350080 | tf_op jit(solution)/shard_map/dot_general | solution.py:83
  522.1 0.3 all-gather.7.cloned.1.call-start
  522.4 0.4 copy-done.24
  522.8 6.1 broadcast_multiply_fusion
  528.9 77.4 %reduce-scatter.11.cloned.1.call-done = f32[1024,1024]{1,0:T(8,128)} async-done(((f32[2048,1024]{1,0:T(8,128)}), f32[1024,1024]{1,0:T(8,128)}) %reduce-scatter.11.cloned.1.call-update) | async-done | bytes 4194320 | tf_op jit(solution)/shard_map/reduce_scatter | solution.py:122
  606.3 4.4 multiply_reduce_fusion.5
  610.7 52.8 %reduce-scatter.7.cloned.1.call-done = bf16[1024,1024]{1,0:T(8,128)(2,1)} async-done(((bf16[2048,1024]{1,0:T(8,128)(2,1)}), bf16[1024,1024]{1,0:T(8,128)(2,1)}) %reduce-scatter.7.cloned.1.call-update) | async-done | bytes 2097168 | tf_op jit(solution)/shard_map/reduce_scatter | solution.py:94
  663.4 10.1 add_convert_fusion
  673.6 0.0 all-gather.11.cloned.1.call-start
  673.6 15.6 %fusion.21 = f32[1024,2304]{1,0:T(8,128)} fusion(bf16[2048,1024]{1,0:T(8,128)(2,1)} %all-gather.5.cloned.1.call-done, bf16[2048,2304]{1,0:T(8,128)(2,1)} %get-tuple-element.35), kind=kOutput, calls=%fused_computation.66 | convolution fusion | flops 9663676416 | bytes 23068672 | tf_op jit(solution)/shard_map/td,tf->df/dot_general | solution.py:88
  689.2 14.1 fusion.22
  703.5 16.4 %fusion.23 = f32[2304,1024]{1,0:T(8,128)} fusion(bf16[2048,2304]{1,0:T(8,128)(2,1)} %get-tuple-element.36, bf16[2048,1024]{1,0:T(8,128)(2,1)} %param.12), kind=kOutput, calls=%fused_computation.68 | convolution fusion | flops 9663676416 | bytes 23068672 | tf_op jit(solution)/shard_map/tf,td->fd/dot_general | solution.py:84
  719.9 3.7 fusion.20
  723.6 1.1 copy-done.14
  724.7 9.8 fusion.4
  734.6 5.0 all-reduce.6
  739.6 60.0 %all-reduce.4 = (f32[1024]{0:T(1024)}, f32[3,512]{1,0:T(4,128)}, f32[1024]{0:T(1024)}) all-reduce(f32[1024]{0:T(1024)S(1)} %get-tuple-element.25, f32[3,512]{1,0:T(4,128)S(1)} %pad_maximum_fusion.3, f32[1024]{0:T(1024)S(1)} %get-tuple-element.26), channel_id=1, replica_groups=mesh['dp'=16,'tensor'=2] {'dp'}, use_global_device_ids=true, to_apply=%region_12.13 | all-reduce | flops 3584 | bytes 28672 | tf_op jit(solution)/shard_map/psum | solution.py:128
  799.6 618.5 %all-reduce.9.cloned.1.call-done = (f32[1024,3,512]{2,0,1:T(8,128)}, f32[512,1024]{1,0:T(8,128)}, f32[1024,2304]{1,0:T(8,128)}, f32[1024,2304]{1,0:T(8,128)}, f32[2304,1024]{1,0:T(8,128)}) async-done(((f32[1024,3,512]{2,0,1:T(8,128)}, f32[512,1024]{1,0:T(8,128)}, f32[1024,2304]{1,0:T(8,128)}, f32[1024,2304]{1,0:T(8,128)}, f32[2304,1024]{1,0:T(8,128)}), (f32[1024,3,512]{2,0,1:T(8,128)}, ...) | async-done | bytes 36700176 | tf_op jit(solution)/shard_map/psum | solution.py:128
  1418.1 4.9 copy.32
  1423.0 2.1 copy.33
  1425.2 1.5 slice-done.7
  1426.7 2.8 copy.34
  1429.5 0.3 copy-done.15
  1429.8 1.3 copy.35
  1431.1 8.4 copy.36
  1439.5 8.1 copy.37
  1447.6 3.7 copy.38
  (117 shorter events, 0.7 us)
Async XLA Ops:
  7.2 4.4 copy-start
  7.2 139.3 %reduce-scatter.5.cloned.1.call-start = ((), (), s32[]{:S(2)}) async-start(), calls=%async_computation.4 | async-start | bytes 12582912 | tf_op jit(solution)/shard_map/reduce_scatter | solution.py:72
  7.2 4.4 copy-start.4
  8.1 10.5 copy-start.26
  11.6 6.9 copy-start.23
  18.6 4.5 copy-start.3
  23.1 3.0 copy-start.38
  23.1 3.3 copy-start.34
  26.4 10.8 copy-start.19
  26.4 10.8 copy-start.21
  26.4 10.7 copy-start.28
  26.4 10.7 copy-start.30
  26.5 10.7 copy-start.32
  26.5 12.1 copy-start.18
  37.2 1.3 copy-start.16
  44.4 6.9 copy-start.35
  44.4 166.8 %all-gather.5.cloned.1.call-start = ((), (), s32[]{:S(2)}) async-start(), calls=%async_computation.5 | async-start | bytes 6291456 | tf_op jit(solution)/shard_map/all_gather | solution.py:77
  150.5 2.0 copy-start.1
  154.3 255.9 %reduce-scatter.9.cloned.1.call-start = ((), (), s32[]{:S(2)}) async-start(), calls=%async_computation.8 | async-start | bytes 12582912 | tf_op jit(solution)/shard_map/reduce_scatter | solution.py:98
  211.2 16.9 %copy-start.36 = (bf16[2048,1024]{1,0:T(8,128)(2,1)S(1)}, bf16[2048,1024]{1,0:T(8,128)(2,1)}, u32[]{:S(2)}) copy-start(bf16[2048,1024]{1,0:T(8,128)(2,1)} %all-gather.5.cloned.1.call-done) | copy-start | bytes 12582916
  279.0 16.1 %copy-start.39 = (bf16[2048,2304]{1,0:T(8,128)(2,1)S(1)}, bf16[2048,2304]{1,0:T(8,128)(2,1)}, u32[]{:S(2)}) copy-start(bf16[2048,2304]{1,0:T(8,128)(2,1)} %get-tuple-element.34) | copy-start | bytes 28311556
  310.8 165.9 %all-gather.9.cloned.1.call-start = ((), (), s32[]{:S(2)}) async-start(), calls=%async_computation.9 | async-start | bytes 6291456 | tf_op jit(solution)/shard_map/all_gather | solution.py:101
  410.2 4.7 copy-start.2
  410.2 5.9 copy-start.6
  416.1 3.7 copy-start.22
  416.1 3.8 copy-start.20
  419.8 186.4 %reduce-scatter.11.cloned.1.call-start = ((), (), s32[]{:S(2)}) async-start(), calls=%async_computation.10 | async-start | bytes 12582912 | tf_op jit(solution)/shard_map/reduce_scatter | solution.py:122
  476.7 14.4 slice-start
  476.7 14.4 slice-start.1
  490.0 2.2 slice-start.2
  490.6 1.7 copy-start.29
  490.6 1.7 copy-start.31
  490.6 1.6 copy-start.33
  495.5 2.5 copy-start.9
  495.5 2.5 copy-start.11
  496.7 1.3 copy-start.13
  506.9 156.6 %reduce-scatter.7.cloned.1.call-start = ((), (), s32[]{:S(2)}) async-start(), calls=%async_computation.6 | async-start | bytes 6291456 | tf_op jit(solution)/shard_map/reduce_scatter | solution.py:94
  522.1 0.7 copy-start.24
  522.1 277.5 %all-gather.7.cloned.1.call-start = ((), (), s32[]{:S(2)}) async-start(), calls=%async_computation.7 | async-start | bytes 6291456 | tf_op jit(solution)/shard_map/all_gather | solution.py:97
  522.8 83.5 %copy-start.27 = (f32[1024]{0:T(1024)S(1)}, f32[1024]{0:T(1024)}, u32[]{:S(2)}) copy-start(f32[1024]{0:T(1024)} %copy-done.26) | copy-start | bytes 12292
  528.9 134.6 %dynamic-slice-start = ((f32[2048]{0:T(1024)}, s32[]{:T(128)}), f32[1024]{0:T(1024)S(1)}, s32[]{:S(2)}) async-start(f32[2048]{0:T(1024)} %copy-done.23, s32[]{:T(128)} %select_n.10), calls=%async_computation.21 | async-start | bytes 8704 | tf_op jit(solution)/shard_map/dynamic-slice
  673.6 126.0 %all-gather.11.cloned.1.call-start = ((), (), s32[]{:S(2)}) async-start(), calls=%async_computation.11 | async-start | bytes 6291456 | tf_op jit(solution)/shard_map/all_gather | solution.py:126
  673.6 15.6 %copy-start.37 = (bf16[2048,1024]{1,0:T(8,128)(2,1)S(1)}, bf16[2048,1024]{1,0:T(8,128)(2,1)}, u32[]{:S(2)}) copy-start(bf16[2048,1024]{1,0:T(8,128)(2,1)} %all-gather.5.cloned.1.call-done) | copy-start | bytes 12582916
  703.4 714.7 %all-reduce.9.cloned.1.call-start = ((), (), s32[]{:S(2)}) async-start(), calls=%async_computation.12 | async-start | bytes 73400320 | tf_op jit(solution)/shard_map/psum | solution.py:128
  703.4 16.4 %copy-start.8 = (bf16[2048,1024]{1,0:T(8,128)(2,1)S(1)}, bf16[2048,1024]{1,0:T(8,128)(2,1)}, u32[]{:S(2)}) copy-start(bf16[2048,1024]{1,0:T(8,128)(2,1)} %all-gather.9.cloned.1.call-done) | copy-start | bytes 12582916
  703.4 16.4 %copy-start.17 = (bf16[2048,512]{1,0:T(8,128)(2,1)S(1)}, bf16[2048,512]{1,0:T(8,128)(2,1)}, u32[]{:S(2)}) copy-start(bf16[2048,512]{1,0:T(8,128)(2,1)} %copy-done.16) | copy-start | bytes 6291460
  719.9 3.7 copy-start.5
  719.9 3.7 copy-start.10
  719.9 3.7 copy-start.12
  719.9 4.8 copy-start.14
  719.9 4.8 copy-start.25
  1418.1 4.9 copy-start.7
  1418.1 7.1 slice-start.6
  1423.0 3.6 slice-start.7
  1426.7 3.1 copy-start.15
  1431.1 16.5 %slice-start.3 = ((s8[9437184]{0:T(1024)(128)(4,1)}), s8[4194304]{0:T(1024)(128)(4,1)S(1)}, s32[]{:S(2)}) async-start(s8[9437184]{0:T(1024)(128)(4,1)} %bitcast.82), calls=%async_computation.16 | async-start | bytes 8388608
  1431.1 16.5 %slice-start.4 = ((s8[9437184]{0:T(1024)(128)(4,1)}), s8[4194304]{0:T(1024)(128)(4,1)S(1)}, s32[]{:S(2)}) async-start(s8[9437184]{0:T(1024)(128)(4,1)} %bitcast.82), calls=%async_computation.17 | async-start | bytes 8388608
  1439.5 8.1 slice-start.5
Sparse Core Ops, SparseCore 0:
  44.5 101.9 reduce-scatter.4
  154.4 56.7 all-gather.4
  310.9 99.2 reduce-scatter.8
  419.9 56.7 all-gather.8
  507.0 99.2 reduce-scatter.10
  609.1 54.3 reduce-scatter.6
  673.7 56.7 all-gather.6
  732.6 56.7 all-gather.10
  795.8 622.2 all-reduce.8
where the time goes:
time: 1470 us; the launch traced here: 1460 us
  waiting for transfers between devices  1060 us (72%)
  matrix products  209 us (14%)
  other arithmetic  65.2 us (4%)
  blocking collectives  65 us (4%)
  local copies, waits for them, and re-layouts  46.5 us (3%)
  between operations  14.8 us (1%)
    psum x1, waiting for transfers between devices, body(): lax.psum((g1_grad, in_grad_w, conv_grad, out_grad, g2_grad, gate_grad, up...  619 us
    reduce_scatter x1, waiting for transfers between devices, body(): lax.psum_scatter(dh2_part, 'tensor', scatter_dimension=0, tiled=True)  99.3 us
    reduce_scatter x1, waiting for transfers between devices, body(): lax.psum_scatter(mix_part, 'tensor', scatter_dimension=0, tiled=True)  95.2 us
    reduce_scatter x1, waiting for transfers between devices, body(): lax.psum_scatter(dh1_part, 'tensor', scatter_dimension=0, tiled=True)  77.4 us
    psum x1, blocking collectives, body(): lax.psum((g1_grad, in_grad_w, conv_grad, out_grad, g2_grad, gate_grad, up...  60 us
    all_gather x1, waiting for transfers between devices, body(): lax.all_gather((normed2 * g2).astype(jnp.bfloat16), 'tensor', axis=0, til...  56.9 us
    all_gather x1, waiting for transfers between devices, body(): lax.all_gather(dr1.astype(jnp.bfloat16), 'tensor', axis=0, tiled=True)  56.7 us
    reduce_scatter x1, waiting for transfers between devices, body(): lax.psum_scatter(ffn_part.astype(jnp.bfloat16), 'tensor', scatter_dimensi...  52.8 us
  transfers between devices with their start and end apart: 9, of which 7 were waited for; matrix products, arithmetic and copies ran while one was open for 6% of the time, Pallas kernels for 0%

commit v1 on v0

--- a/solution.py
+++ b/solution.py
@@ -4,6 +4,8 @@
 from jax.sharding import PartitionSpec as P
 
 EPS = 1e-05
+F32 = jnp.float32
+BF = jnp.bfloat16
 
 
 def distances(lengths, count):
@@ -31,6 +33,151 @@
     weighted = grad_in * gain
     inner = jnp.mean(weighted * normed, axis=-1, keepdims=True)
     return (scale * (weighted - normed * inner), jnp.sum(grad_in * normed, axis=0))
+
+
+def dot(a, b, ca, cb):
+    return lax.dot_general(a, b, (((ca,), (cb,)), ((), ())), preferred_element_type=F32)
+
+
+def swap_tensor(value):
+    return lax.ppermute(value, "tensor", [(0, 1), (1, 0)])
+
+
+def swap_core(value, count):
+    return lax.ppermute(value, "dp", [(i, i ^ 1) for i in range(count)])
+
+
+def fetch_other(weight, core, count):
+    half = weight.shape[0] // 2
+    mine = lax.dynamic_slice_in_dim(weight, core * half, half, 0)
+    got = swap_tensor(mine)
+    rest = swap_core(got, count)
+    low = jnp.where(core == 0, got, rest)
+    high = jnp.where(core == 0, rest, got)
+    return jnp.concatenate([low, high], 0)
+
+
+def pair_body(
+    tokens,
+    cotangent,
+    lengths,
+    mixer_gain,
+    in_weight,
+    conv_weight,
+    out_weight,
+    ffn_gain,
+    gate_weight,
+    up_weight,
+    down_weight,
+):
+    rows, width = tokens.shape
+    count = lax.axis_size("dp")
+    core = lax.axis_index("dp") % 2
+    side = lax.axis_index("tensor")
+    half = out_weight.shape[0]
+    in_flat = in_weight.reshape(width, 3 * half)
+    in_other = fetch_other(in_flat, core, count).reshape(width, 3, half)
+    out_other = fetch_other(out_weight, core, count)
+    taps_other = swap_tensor(conv_weight)
+
+    def ordered(own, other, axis):
+        return jnp.concatenate(
+            [jnp.where(side == 0, own, other), jnp.where(side == 0, other, own)], axis
+        )
+
+    in_full = ordered(in_weight, in_other, 2).reshape(width, 6 * half)
+    out_full = ordered(out_weight, out_other, 0)
+    taps = ordered(conv_weight, taps_other, 1).astype(F32)
+    full = 2 * half
+
+    dist = distances(lengths[0], rows)
+    keep_one = (dist >= 1)[:, None].astype(F32)
+    keep_two = (dist >= 2)[:, None].astype(F32)
+    x = tokens.astype(F32)
+    dy = cotangent.astype(F32)
+    g1 = mixer_gain.astype(F32)
+    g2 = ffn_gain.astype(F32)
+    scale1 = rms_scale(x)
+    normed1 = x * scale1
+    h1b = (normed1 * g1).astype(BF)
+    proj = dot(h1b, in_full, 1, 0)
+    b_part, c_part, x_part = (proj[:, :full], proj[:, full : 2 * full], proj[:, 2 * full :])
+    mixed = b_part * x_part
+    mixed_one = shift_down(mixed, 1, keep_one)
+    mixed_two = shift_down(mixed, 2, keep_two)
+    conv_out = taps[0] * mixed + taps[1] * mixed_one + taps[2] * mixed_two
+    zb = (c_part * conv_out).astype(BF)
+    resid = x + dot(zb, out_full, 1, 0)
+    scale2 = rms_scale(resid)
+    normed2 = resid * scale2
+    h2b = (normed2 * g2).astype(BF)
+
+    gate = dot(h2b, gate_weight, 1, 0)
+    up = dot(h2b, up_weight, 1, 0)
+    sig = jax.nn.sigmoid(gate)
+    silu = gate * sig
+    hidb = (silu * up).astype(BF)
+    down_grad = dot(hidb, cotangent, 0, 0).astype(BF)
+    down_sum = lax.psum(down_grad, "dp")
+    d_hid = dot(cotangent, down_weight, 1, 1)
+    d_gate = (d_hid * up * sig * (1.0 + gate * (1.0 - sig))).astype(BF)
+    d_up = (d_hid * silu).astype(BF)
+    dh2_own = (dot(d_gate, gate_weight, 1, 1) + dot(d_up, up_weight, 1, 1)).astype(BF)
+    dh2_got = swap_tensor(dh2_own)
+    gate_grad = dot(h2b, d_gate, 0, 0).astype(BF)
+    up_grad = dot(h2b, d_up, 0, 0).astype(BF)
+    gate_sum, up_sum = lax.psum((gate_grad, up_grad), "dp")
+    ffn_own = dot(hidb, down_weight, 1, 0).astype(BF)
+    ffn_got = swap_tensor(ffn_own)
+
+    dh2 = dh2_own.astype(F32) + dh2_got.astype(F32)
+    d_resid, g2_grad = norm_back(dh2, normed2, scale2, g2)
+    dr1 = dy + d_resid
+    dr1b = dr1.astype(BF)
+    own = lambda v, axis: lax.dynamic_slice_in_dim(v, side * half, half, axis)
+    out_grad = dot(own(zb, 1), dr1b, 0, 0).astype(BF)
+    d_z = dot(dr1b, out_full, 1, 1)
+    d_c = d_z * conv_out
+    d_conv = d_z * c_part
+    d_own = own(d_conv, 1)
+    conv_grad = jnp.stack(
+        [
+            jnp.sum(d_own * own(mixed, 1), axis=0),
+            jnp.sum(d_own * own(mixed_one, 1), axis=0),
+            jnp.sum(d_own * own(mixed_two, 1), axis=0),
+        ],
+        0,
+    )
+    d_mixed = (
+        taps[0] * d_conv
+        + taps[1] * shift_up(d_conv * keep_one, 1)
+        + taps[2] * shift_up(d_conv * keep_two, 2)
+    )
+    d_b = (d_mixed * x_part).astype(BF)
+    d_c = d_c.astype(BF)
+    d_x = (d_mixed * b_part).astype(BF)
+    in_grad = jnp.stack(
+        [dot(h1b, own(d_b, 1), 0, 0), dot(h1b, own(d_c, 1), 0, 0), dot(h1b, own(d_x, 1), 0, 0)], 1
+    ).astype(BF)
+    d_proj = jnp.concatenate([d_b, d_c, d_x], 1)
+    dh1 = dot(d_proj, in_full, 1, 1)
+    d_input, g1_grad = norm_back(dh1, normed1, scale1, g1)
+    input_grad = (dr1 + d_input).astype(BF)
+    output = (resid + (ffn_own.astype(F32) + ffn_got.astype(F32))).astype(BF)
+    in_sum, out_sum = lax.psum((in_grad, out_grad), "dp")
+    g1_sum, conv_sum, g2_sum = lax.psum((g1_grad, conv_grad, g2_grad), "dp")
+    return (
+        output,
+        input_grad,
+        g1_sum,
+        in_sum.astype(F32),
+        conv_sum,
+        out_sum.astype(F32),
+        g2_sum,
+        gate_sum.astype(F32),
+        up_sum.astype(F32),
+        down_sum.astype(F32),
+    )
 
 
 def body(
@@ -143,8 +290,9 @@
 
 
 def solution(mesh):
+    paired = mesh.shape["tensor"] == 2 and mesh.shape["dp"] % 2 == 0
     return jax.shard_map(
-        body,
+        pair_body if paired else body,
         mesh=mesh,
         in_specs=(
             P("dp", None),

time: 1470 us -> 890 us (0.61)
  waiting for transfers between devices: 1060 us -> 377 us
  other arithmetic: 65.2 us -> 147 us
  matrix products: 209 us -> 228 us
    psum x1, waiting for transfers between devices: 619 us -> 212 us  [pair_body(): in_sum, out_sum = lax.psum((in_grad, out_grad), 'dp')]
    reduce_scatter x4 -> x0, waiting for transfers between devices: 325 us -> none  [the longest x1 99.3 us: body(): lax.psum_scatter(dh2_part, 'tensor', scatter_dimension=0, tiled=True)]
    ppermute x0 -> x7, waiting for transfers between devices: none -> 165 us  [the longest x5 165 us: swap_tensor(): return lax.ppermute(value, 'tensor', [(0, 1), (1, 0)])]
    all_gather x4 -> x0, waiting for transfers between devices: 114 us -> none  [the longest x1 56.9 us: body(): lax.all_gather((normed2 * g2).astype(jnp.bfloat16), 'tensor', axis=0, til...]
    convert_element_type x8 -> x13, other arithmetic: 33.6 us -> 83.5 us  [the longest x1 28 us: pair_body(): zb = (c_part * conv_out).astype(BF)]
    dot_general x15 -> x17, matrix products: 209 us -> 228 us  [dot(): lax.dot_general(a, b, (((ca,), (cb,)), ((), ())), preferred_element_type=...]
    unnamed x103 -> x109, local copies, waits for them, and re-layouts: 46.3 us -> 37.2 us
    psum x2 -> x1, blocking collectives: 65 us -> 65.4 us  [pair_body(): g1_sum, conv_sum, g2_sum = lax.psum((g1_grad, conv_grad, g2_grad), 'dp')]
  transfers between devices with their start and end apart: 9 -> 8, of which waited for: 7 -> 5; matrix products, arithmetic and copies ran while one was open for 6% -> 14% of each run, Pallas kernels for 0% -> 0%
where the time goes in v1:
time: 890 us; the launch traced here: 882 us
  waiting for transfers between devices  377 us (42%)
  matrix products  228 us (26%)
  other arithmetic  147 us (17%)
  blocking collectives  65.4 us (7%)
  local copies, waits for them, and re-layouts  41.7 us (5%)
  between operations  15.2 us (2%)
    dot_general x17, matrix products, dot(): lax.dot_general(a, b, (((ca,), (cb,)), ((), ())), preferred_element_type=...  228 us
    psum x1, waiting for transfers between devices, pair_body(): in_sum, out_sum = lax.psum((in_grad, out_grad), 'dp')  212 us
    ppermute x5, waiting for transfers between devices, swap_tensor(): return lax.ppermute(value, 'tensor', [(0, 1), (1, 0)])  165 us
    psum x1, blocking collectives, pair_body(): g1_sum, conv_sum, g2_sum = lax.psum((g1_grad, conv_grad, g2_grad), 'dp')  65.4 us
    unnamed x109, local copies, waits for them, and re-layouts  37.2 us
    convert_element_type x1, other arithmetic, pair_body(): zb = (c_part * conv_out).astype(BF)  28 us
  transfers between devices with their start and end apart: 8, of which 5 were waited for; matrix products, arithmetic and copies ran while one was open for 14% of the time, Pallas kernels for 0%

profile of v1, /device:TPU:0, one launch (start us, length us, event | category | flops | bytes accessed | tf_op | source)
XLA Modules:
  0.0 881.5 jit_solution(9237847768362746972)
XLA Ops:
  7.3 3.2 copy.44
  10.5 1.3 constant_dynamic-slice_fusion.1
  11.8 2.9 collective-permute-start
  14.8 1.9 constant_dynamic-slice_fusion
  16.6 2.0 collective-permute-start.3
  18.6 0.2 reduce-window_clone.1
  18.9 31.3 %collective-permute-done = bf16[512,1536]{0,1:T(8,128)(2,1)} collective-permute-done((bf16[512,1536]{0,1:T(8,128)(2,1)}, bf16[512,1536]{0,1:T(8,128)(2,1)}, u32[]{:S(2)}, u32[]{:S(2)}) %collective-permute-start) | collective-permute-done | bytes 1572896 | tf_op jit(solution)/shard_map/ppermute | solution.py:43
  50.3 6.4 copy.42
  56.7 3.1 fusion.18
  59.8 1.0 collective-permute-done.3
  60.9 6.4 copy.47
  67.3 0.7 slice.49
  68.0 0.7 slice.51
  68.7 1.3 broadcast_select_fusion.7
  70.0 3.1 broadcast_select_fusion.5
  73.1 2.1 broadcast_select_fusion.3
  75.2 0.4 pad_maximum_fusion.1
  75.6 0.4 broadcast_select_fusion.1
  76.1 3.4 pad_maximum_fusion
  79.5 20.2 %fusion.65 = f32[2048,3072]{1,0:T(8,128)} fusion(bf16[1024,3072]{0,1:T(8,128)(2,1)} %bitcast.46, bf16[2048,1024]{0,1:T(8,128)(2,1)S(1)} %copy-done.3, f32[1024]{0:T(1024)S(1)} %convert_element_type.114, f32[2048]{0:T(1024)S(1)} %add_rsqrt_fusion.1), kind=kOutput, calls=%fused_computation.111 | convolution fusion | flops 12893290496 | bytes 35663872 | tf_op jit(solution)/shard_map/dot_general | solution.py:39
  99.7 12.0 %slice_multiply_fusion.2 = f32[2048,1024]{1,0:T(8,128)} fusion(f32[2048,3072]{1,0:T(8,128)} %fusion.65), kind=kLoop, calls=%fused_computation.45 | loop fusion | flops 2097152 | bytes 25165824 | tf_op jit(solution)/shard_map/mul | solution.py:105
  111.7 28.0 %multiply_convert_fusion.7 = (bf16[2048,1024]{1,0:T(8,128)(2,1)}, f32[2048,1024]{1,0:T(8,128)}, f32[2048,1024]{1,0:T(8,128)}, f32[2048,1024]{1,0:T(8,128)}) fusion(f32[2048,3072]{1,0:T(8,128)} %fusion.65, f32[1024]{0:T(1024)S(1)} %bitcast.56, f32[1024]{0:T(1024)S(1)} %bitcast.54, f32[1024]{0:T(1024)S(1)} %bitcast.52, f32[2048]{0:T(1024)S(1)} %get-tuple-element.77, ...), kind=kLoop, calls=%fused_computation.40 | loop fusion | flops 20971520 | bytes 71319552 | tf_op jit(solution)/shard_map/convert_element_type | solution.py:109
  139.7 7.3 multiply_reduce_fusion.2
  147.1 0.7 multiply_convert_fusion.6
  147.9 0.6 slice-done.6
  148.5 4.0 slice-done.7
  152.5 13.6 %fusion.67 = f32[2048,2304]{1,0:T(8,128)} fusion(bf16[2048,1024]{0,1:T(8,128)(2,1)S(1)} %multiply_convert_fusion.6, bf16[1024,2304]{1,0:T(8,128)(2,1)S(1)} %bitcast.62), kind=kOutput, calls=%fused_computation.112 | convolution fusion | flops 9663676416 | bytes 27787264 | tf_op jit(solution)/shard_map/dot_general | solution.py:39
  166.1 14.1 %fusion.68 = f32[2048,2304]{1,0:T(8,128)} fusion(bf16[2048,1024]{0,1:T(8,128)(2,1)S(1)} %multiply_convert_fusion.6, bf16[1024,2304]{1,0:T(8,128)(2,1)S(1)} %bitcast.64), kind=kOutput, calls=%fused_computation.113 | convolution fusion | flops 9663676416 | bytes 27787264 | tf_op jit(solution)/shard_map/dot_general | solution.py:39
  180.2 35.4 %multiply_convert_fusion = (bf16[2048,2304]{1,0:T(8,128)(2,1)}, bf16[2048,2304]{1,0:T(8,128)(2,1)}, bf16[2048,2304]{1,0:T(8,128)(2,1)}) fusion(f32[2048,2304]{1,0:T(8,128)} %fusion.67, f32[2048,2304]{1,0:T(8,128)} %fusion.68, bf16[2048,1024]{1,0:T(8,128)(2,1)} %param.12, bf16[2304,1024]{1,0:T(8,128)(2,1)} %param.21), kind=kOutput, calls=%fused_computation | convolution fusion | flops 9734455296 | bytes 74973184 | tf_op jit(solution)/shard_map/dot_general | solution.py:39
  215.6 16.2 %convolution_convert_fusion.1 = bf16[1024,2304]{1,0:T(8,128)(2,1)} fusion(bf16[2048,1024]{0,1:T(8,128)(2,1)} %copy-done.10, bf16[2048,2304]{1,0:T(8,128)(2,1)} %get-tuple-element.61), kind=kOutput, calls=%fused_computation.49 | convolution fusion | flops 9666035712 | bytes 18350080 | tf_op jit(solution)/shard_map/dot_general | solution.py:39
  231.8 13.8 %fusion.69 = f32[2048,1024]{0,1:T(8,128)} fusion(bf16[2048,2304]{1,0:T(8,128)(2,1)S(1)} %copy-done.38, bf16[1024,2304]{1,0:T(8,128)(2,1)} %param.19), kind=kOutput, calls=%fused_computation.114 | convolution fusion | flops 9663676416 | bytes 22544384 | tf_op jit(solution)/shard_map/dot_general | solution.py:39
  245.7 13.1 %add_convert_fusion = bf16[2048,1024]{0,1:T(8,128)(2,1)S(1)} fusion(f32[2048,1024]{0,1:T(8,128)} %fusion.69, bf16[2048,2304]{1,0:T(8,128)(2,1)S(1)} %bitcast.66, bf16[1024,2304]{1,0:T(8,128)(2,1)} %param.20), kind=kOutput, calls=%fused_computation.36 | convolution fusion | flops 9667870720 | bytes 26738688 | tf_op jit(solution)/shard_map/dot_general | solution.py:39
  258.8 1.8 collective-permute-start.6
  260.6 14.2 %convolution_convert_fusion.3 = bf16[2048,1024]{0,1:T(8,128)(2,1)S(1)} fusion(bf16[2048,2304]{1,0:T(8,128)(2,1)} %get-tuple-element.63, bf16[2304,1024]{1,0:T(8,128)(2,1)} %param.21), kind=kOutput, calls=%fused_computation.54 | convolution fusion | flops 9665773568 | bytes 18350080 | tf_op jit(solution)/shard_map/dot_general | solution.py:39
  274.8 0.3 collective-permute-start.5
  275.2 16.9 %convolution_convert_fusion = bf16[2304,1024]{1,0:T(8,128)(2,1)} fusion(bf16[2048,2304]{1,0:T(8,128)(2,1)} %get-tuple-element.63, bf16[2048,1024]{1,0:T(8,128)(2,1)} %param.12), kind=kOutput, calls=%fused_computation.48 | convolution fusion | flops 9666035712 | bytes 18350080 | tf_op jit(solution)/shard_map/dot_general | solution.py:39
  292.1 14.0 %convolution_convert_fusion.2 = bf16[1024,2304]{1,0:T(8,128)(2,1)} fusion(bf16[2048,1024]{0,1:T(8,128)(2,1)S(1)} %copy-done.11, bf16[2048,2304]{1,0:T(8,128)(2,1)} %get-tuple-element.62), kind=kOutput, calls=%fused_computation.50 | convolution fusion | flops 9666035712 | bytes 18350080 | tf_op jit(solution)/shard_map/dot_general | solution.py:39
  306.1 46.2 %collective-permute-done.6 = bf16[2048,1024]{0,1:T(8,128)(2,1)S(1)} collective-permute-done((bf16[2048,1024]{0,1:T(8,128)(2,1)S(1)}, bf16[2048,1024]{0,1:T(8,128)(2,1)S(1)}, u32[]{:S(2)}, u32[]{:S(2)}) %collective-permute-start.6) | collective-permute-done | bytes 4194336 | tf_op jit(solution)/shard_map/ppermute | solution.py:43
  352.3 3.3 multiply_reduce_fusion
  355.6 86.2 %collective-permute-done.5 = bf16[2048,1024]{0,1:T(8,128)(2,1)} collective-permute-done((bf16[2048,1024]{0,1:T(8,128)(2,1)S(1)}, bf16[2048,1024]{0,1:T(8,128)(2,1)}, u32[]{:S(2)}, u32[]{:S(2)}) %collective-permute-start.5) | collective-permute-done | bytes 4194336 | tf_op jit(solution)/shard_map/ppermute | solution.py:43
  441.8 12.6 %multiply_add_fusion.1 = (f32[2048,1024]{0,1:T(8,128)S(1)}, bf16[2048,1024]{0,1:T(8,128)(2,1)}) fusion(bf16[2048,1024]{0,1:T(8,128)(2,1)} %copy.47, bf16[2048,1024]{0,1:T(8,128)(2,1)} %copy-done.6, bf16[2048,1024]{0,1:T(8,128)(2,1)S(1)} %add_convert_fusion, f32[2048,1024]{0,1:T(8,128)} %copy-done.2, f32[2048]{0:T(1024)S(1)} %broadcast_multiply_fusion.1, ...), kind=kLoop, calls=%fused_computation.33 | loop fusion | flops 31457280 | bytes 41963520 | tf_op jit(solution)/shard_map/add | solution.py:135
  454.5 3.5 copy-done.1
  458.0 5.0 fusion.40
  463.0 14.6 %multiply_convert_fusion.4 = (bf16[2048,1024]{1,0:T(8,128)(2,1)}, f32[2048,1024]{1,0:T(8,128)}) fusion(f32[2048,1024]{1,0:T(8,128)} %get-tuple-element.58, f32[2048,3072]{1,0:T(8,128)} %fusion.65, bf16[512,1024]{1,0:T(8,128)(2,1)S(1)} %copy-done.15, bf16[512,1024]{1,0:T(8,128)(2,1)S(1)} %copy-done.13, f32[2048,1024]{0,1:T(8,128)} %copy-done.1), kind=kOutput, calls=%fused_computation.30 | convolution fusion | flops 4307550208 | bytes 39845888 | tf_op jit(solution)/shard_map/dot_general | solution.py:39
  477.6 7.7 slice_multiply_fusion.1
  485.3 4.2 slice_multiply_fusion
  489.6 14.5 %multiply_convert_fusion.5 = (bf16[2048,1024]{1,0:T(8,128)(2,1)}, f32[2048,1024]{1,0:T(8,128)}) fusion(f32[2048,3072]{1,0:T(8,128)} %fusion.65, f32[2046,1024]{1,0:T(8,128)} %slice_multiply_fusion, f32[1024]{0:T(1024)S(1)} %bitcast.57, f32[2047,1024]{1,0:T(8,128)} %slice_multiply_fusion.1, f32[1024]{0:T(1024)S(1)} %bitcast.55, f32[2048,1024]{1,0:T(8,128)S(1)} %copy-done, ...), kind=kLoop, calls=%fused_computation.31 | loop fusion | flops 14680064 | bytes 46137344 | tf_op jit(solution)/shard_map/convert_element_type | solution.py:156
  504.1 9.5 %multiply_convert_fusion.3 = bf16[2048,1024]{1,0:T(8,128)(2,1)} fusion(f32[2048,1024]{1,0:T(8,128)} %get-tuple-element.56, f32[2048,3072]{1,0:T(8,128)} %fusion.65), kind=kLoop, calls=%fused_computation.29 | loop fusion | flops 4194304 | bytes 20971520 | tf_op jit(solution)/shard_map/convert_element_type | solution.py:158
  513.6 4.1 fusion.45
  517.8 2.4 fusion.51
  520.2 2.4 fusion.48
  522.6 2.0 pad_maximum_fusion.2
  524.6 20.9 %fusion.17 = (f32[1024]{0:T(1024)S(1)}, f32[2048]{0:T(1024)S(1)}, f32[2048,1024]{0,1:T(8,128)}) fusion(bf16[2048,1024]{0,1:T(8,128)(2,1)} %copy.42, f32[2048]{0:T(1024)S(1)} %copy-done.29, f32[1024]{0:T(1024)S(1)} %copy-done.33, bf16[1024,3072]{0,1:T(8,128)(2,1)} %bitcast.47, bf16[2048,1024]{1,0:T(8,128)(2,1)} %multiply_convert_fusion.3, ...), kind=kOutput, calls=%fused_computation.24 | convolution fusion | flops 12937327616 | bytes 31481856 | tf_op jit(solution)/shard_map/dot_general | solution.py:39
  545.6 9.0 %fusion.16 = bf16[2048,1024]{0,1:T(8,128)(2,1)} fusion(f32[2048,1024]{0,1:T(8,128)} %copy-done.1, bf16[2048,1024]{0,1:T(8,128)(2,1)S(1)} %copy-done.5, f32[2048,1024]{0,1:T(8,128)} %get-tuple-element.85, f32[2048]{0:T(1024)S(1)} %broadcast_multiply_fusion, f32[1024]{0:T(1024)S(1)} %copy-done.33, f32[2048]{0:T(1024)S(1)} %copy-done.29), kind=kLoop, calls=%fused_computation.23 | loop fusion | flops 16777216 | bytes 25186304 | tf_op jit(solution)/shard_map/convert_element_type | solution.py:165
  554.6 6.4 copy.53
  561.0 6.4 copy.52
  567.4 7.8 multiply_reduce_fusion.5
  575.2 65.4 %all-reduce.4 = (f32[1024]{0:T(1024)}, f32[3,512]{1,0:T(4,128)}, f32[1024]{0:T(1024)}) all-reduce(f32[1024]{0:T(1024)S(1)} %get-tuple-element.42, f32[3,512]{1,0:T(4,128)S(1)} %pad_maximum_fusion.7, f32[1024]{0:T(1024)S(1)} %get-tuple-element.40), channel_id=1, replica_groups=mesh['dp'=16,'tensor'=2] {'dp'}, use_global_device_ids=true, to_apply=%region_7.8 | all-reduce | flops 3584 | bytes 28672 | tf_op jit(solution)/shard_map/psum | solution.py:168
  640.6 211.9 %all-reduce.8.cloned.1.call-done = (bf16[1024,3,512]{2,0,1:T(8,128)(2,1)}, bf16[512,1024]{1,0:T(8,128)(2,1)}, bf16[1024,2304]{1,0:T(8,128)(2,1)}, bf16[1024,2304]{1,0:T(8,128)(2,1)}, bf16[2304,1024]{1,0:T(8,128)(2,1)}) async-done(((bf16[1024,3,512]{2,0,1:T(8,128)(2,1)}, bf16[512,1024]{1,0:T(8,128)(2,1)}, bf16[1024,2304]{1,0:T(8,128)(2,1)}, bf16[1024,2304]{1,0:T(8,128)(2,1)}, bf16[2304,1024]{1,0:T(8,128)(2,1)}), ...) | async-done | bytes 18350096 | tf_op jit(solution)/shard_map/psum | solution.py:167
  852.5 6.9 convert_element_type.142
  859.4 4.7 convert_element_type.144
  864.1 4.9 convert_element_type.146
  869.0 3.6 convert_element_type.138
  872.6 1.6 convert_element_type.140
  (127 shorter events, 0.5 us)
Async XLA Ops:
  7.2 7.6 copy-start.34
  7.2 11.5 %copy-start.37 = (s32[1,3]{1,0:T(1,128)S(1)}, s32[1,3]{1,0:T(1,128)}, u32[]{:S(2)}) copy-start(s32[1,3]{1,0:T(1,128)} %param.13) | copy-start | bytes 40
  7.2 845.3 %all-reduce.8.cloned.1.call-start = ((), (), s32[]{:S(2)}) async-start(), calls=%async_computation | async-start | bytes 36700160 | tf_op jit(solution)/shard_map/psum | solution.py:167
  10.5 50.3 %copy-start.35 = (bf16[1024]{0:T(1024)(128)(2,1)S(1)}, bf16[1024]{0:T(1024)(128)(2,1)}, u32[]{:S(2)}) copy-start(bf16[1024]{0:T(1024)(128)(2,1)} %param.14) | copy-start | bytes 6148
  10.5 50.4 %copy-start.36 = (bf16[1024]{0:T(1024)(128)(2,1)S(1)}, bf16[1024]{0:T(1024)(128)(2,1)}, u32[]{:S(2)}) copy-start(bf16[1024]{0:T(1024)(128)(2,1)} %param.18) | copy-start | bytes 6148
  11.8 38.5 %collective-permute-start = (bf16[512,1536]{0,1:T(8,128)(2,1)}, bf16[512,1536]{0,1:T(8,128)(2,1)}, u32[]{:S(2)}, u32[]{:S(2)}) collective-permute-start(bf16[512,1536]{0,1:T(8,128)(2,1)} %constant_dynamic-slice_fusion.1), channel_id=1, source_target_pairs={{0,1},{1,0},{2,3},{3,2},{4,5},{5,4},{6,7},{7,6},{8,9},{9,8},{10,11... | collective-permute-start | bytes 4718600 | tf_op jit(solution)/shard_map/ppermute | solution.py:43
  14.7 53.9 %collective-permute-start.2 = (bf16[3,512]{1,0:T(4,128)(2,1)S(1)}, bf16[3,512]{1,0:T(4,128)(2,1)S(1)}, u32[]{:S(2)}, u32[]{:S(2)}) collective-permute-start(bf16[3,512]{1,0:T(4,128)(2,1)S(1)} %copy-done.34), channel_id=1, source_target_pairs={{0,1},{1,0},{2,3},{3,2},{4,5},{5,4},{6,7},{7,6},{8,9},{9,8},{10,11... | collective-permute-start | bytes 9224 | tf_op jit(solution)/shard_map/ppermute | solution.py:43
  16.6 44.1 %collective-permute-start.3 = (bf16[256,1024]{1,0:T(8,128)(2,1)}, bf16[256,1024]{1,0:T(8,128)(2,1)}, u32[]{:S(2)}, u32[]{:S(2)}) collective-permute-start(bf16[256,1024]{1,0:T(8,128)(2,1)} %constant_dynamic-slice_fusion), channel_id=1, source_target_pairs={{0,1},{1,0},{2,3},{3,2},{4,5},{5,4},{6,7},{7,6},{8,9},{9,8},{10,11... | collective-permute-start | bytes 1572872 | tf_op jit(solution)/shard_map/ppermute | solution.py:43
  50.3 22.9 %collective-permute-start.1 = (bf16[512,1536]{0,1:T(8,128)(2,1)}, bf16[512,1536]{0,1:T(8,128)(2,1)}, u32[]{:S(2)}, u32[]{:S(2)}) collective-permute-start(bf16[512,1536]{0,1:T(8,128)(2,1)} %collective-permute-done), channel_id=1, source_target_pairs={{0,2},{2,0},{4,6},{6,4},{8,10},{10,8},{12,14},{14,12},{16,18},{18,... | collective-permute-start | bytes 4718600 | tf_op jit(solution)/shard_map/ppermute | solution.py:47
  60.8 7.9 collective-permute-start.4
  60.8 18.7 %copy-start.28 = (f32[2048]{0:T(1024)}, f32[2048]{0:T(1024)S(1)}, u32[]{:S(2)}) copy-start(f32[2048]{0:T(1024)S(1)} %add_rsqrt_fusion.1) | copy-start | bytes 24580
  60.8 18.7 %copy-start.32 = (f32[1024]{0:T(1024)}, f32[1024]{0:T(1024)S(1)}, u32[]{:S(2)}) copy-start(f32[1024]{0:T(1024)S(1)} %convert_element_type.114) | copy-start | bytes 12292
  60.9 86.3 %copy-start.20 = (f32[1024]{0:T(1024)}, f32[1024]{0:T(1024)S(1)}, u32[]{:S(2)}) copy-start(f32[1024]{0:T(1024)S(1)} %convert_element_type.120) | copy-start | bytes 12292
  68.7 43.0 %copy-start.22 = (f32[1,1024]{1,0:T(1,128)}, f32[1,1024]{1,0:T(1,128)S(1)}, u32[]{:S(2)}) copy-start(f32[1,1024]{1,0:T(1,128)S(1)} %get-tuple-element.78) | copy-start | bytes 12292
  68.7 43.0 %copy-start.24 = (f32[1,1024]{1,0:T(1,128)}, f32[1,1024]{1,0:T(1,128)S(1)}, u32[]{:S(2)}) copy-start(f32[1,1024]{1,0:T(1,128)S(1)} %get-tuple-element.79) | copy-start | bytes 12292
  68.7 43.0 %copy-start.26 = (f32[1,1024]{1,0:T(1,128)}, f32[1,1024]{1,0:T(1,128)S(1)}, u32[]{:S(2)}) copy-start(f32[1,1024]{1,0:T(1,128)S(1)} %get-tuple-element.80) | copy-start | bytes 12292
  76.0 3.5 copy-start.3
  111.7 28.0 %copy-start.12 = (bf16[512,1024]{1,0:T(8,128)(2,1)S(1)}, bf16[512,1024]{1,0:T(8,128)(2,1)}, u32[]{:S(2)}) copy-start(bf16[512,1024]{1,0:T(8,128)(2,1)} %get-tuple-element.72) | copy-start | bytes 3145732
  111.7 28.0 %copy-start.14 = (bf16[512,1024]{1,0:T(8,128)(2,1)S(1)}, bf16[512,1024]{1,0:T(8,128)(2,1)}, u32[]{:S(2)}) copy-start(bf16[512,1024]{1,0:T(8,128)(2,1)} %get-tuple-element.73) | copy-start | bytes 3145732
  147.1 19.0 %copy-start.2 = (f32[2048,1024]{0,1:T(8,128)}, f32[2048,1024]{0,1:T(8,128)S(1)}, u32[]{:S(2)}) copy-start(f32[2048,1024]{0,1:T(8,128)S(1)} %get-tuple-element.84) | copy-start | bytes 25165828
  147.1 1.4 slice-start.6
  147.1 19.0 %copy-start.18 = (f32[2048]{0:T(1024)}, f32[2048]{0:T(1024)S(1)}, u32[]{:S(2)}) copy-start(f32[2048]{0:T(1024)S(1)} %add_rsqrt_fusion) | copy-start | bytes 24580
  147.1 5.3 slice-start.7
  147.1 19.0 %slice-start.8 = ((s8[4718592]{0:T(1024)(128)(4,1)}), s8[4194304]{0:T(1024)(128)(4,1)S(1)}, s32[]{:S(2)}) async-start(s8[4718592]{0:T(1024)(128)(4,1)} %bitcast.63), calls=%async_computation.9 | async-start | bytes 8388608
  152.4 13.6 %copy-start.10 = (bf16[2048,1024]{0,1:T(8,128)(2,1)}, bf16[2048,1024]{0,1:T(8,128)(2,1)S(1)}, u32[]{:S(2)}) copy-start(bf16[2048,1024]{0,1:T(8,128)(2,1)S(1)} %multiply_convert_fusion.6) | copy-start | bytes 12582916
  152.5 13.7 %slice-start.9 = ((s8[4718592]{0:T(1024)(128)(4,1)}), s8[524288]{0:T(1024)(128)(4,1)S(1)}, s32[]{:S(2)}) async-start(s8[4718592]{0:T(1024)(128)(4,1)} %bitcast.63), calls=%async_computation.10 | async-start | bytes 1048576
  215.6 16.2 %copy-start.38 = (bf16[2048,2304]{1,0:T(8,128)(2,1)S(1)}, bf16[2048,2304]{1,0:T(8,128)(2,1)}, u32[]{:S(2)}) copy-start(bf16[2048,2304]{1,0:T(8,128)(2,1)} %get-tuple-element.62) | copy-start | bytes 28311556
  215.6 30.0 %slice-start.10 = ((s8[9437184]{0:T(1024)(128)(4,1)}), s8[4194304]{0:T(1024)(128)(4,1)S(1)}, s32[]{:S(2)}) async-start(s8[9437184]{0:T(1024)(128)(4,1)} %bitcast.65), calls=%async_computation.11 | async-start | bytes 8388608
  215.6 30.0 %slice-start.11 = ((s8[9437184]{0:T(1024)(128)(4,1)}), s8[4194304]{0:T(1024)(128)(4,1)S(1)}, s32[]{:S(2)}) async-start(s8[9437184]{0:T(1024)(128)(4,1)} %bitcast.65), calls=%async_computation.12 | async-start | bytes 8388608
  231.8 13.9 %slice-start.12 = ((s8[9437184]{0:T(1024)(128)(4,1)}), s8[1048576]{0:T(1024)(128)(4,1)S(1)}, s32[]{:S(2)}) async-start(s8[9437184]{0:T(1024)(128)(4,1)} %bitcast.65), calls=%async_computation.13 | async-start | bytes 2097152
  258.8 93.4 %collective-permute-start.6 = (bf16[2048,1024]{0,1:T(8,128)(2,1)S(1)}, bf16[2048,1024]{0,1:T(8,128)(2,1)S(1)}, u32[]{:S(2)}, u32[]{:S(2)}) collective-permute-start(bf16[2048,1024]{0,1:T(8,128)(2,1)S(1)} %add_convert_fusion), channel_id=1, source_target_pairs={{0,1},{1,0},{2,3},{3,2},{4,5},{5,4},{6,7},{7,6},{8,9},{9,8},{10,11... | collective-permute-start | bytes 12582920 | tf_op jit(solution)/shard_map/ppermute | solution.py:43
  274.8 17.2 %copy-start.9 = (bf16[2048,1024]{0,1:T(8,128)(2,1)}, bf16[2048,1024]{0,1:T(8,128)(2,1)S(1)}, u32[]{:S(2)}) copy-start(bf16[2048,1024]{0,1:T(8,128)(2,1)S(1)} %convolution_convert_fusion.3) | copy-start | bytes 12582916
  274.8 17.2 %copy-start.11 = (bf16[2048,1024]{0,1:T(8,128)(2,1)S(1)}, bf16[2048,1024]{0,1:T(8,128)(2,1)}, u32[]{:S(2)}) copy-start(bf16[2048,1024]{0,1:T(8,128)(2,1)} %copy-done.10) | copy-start | bytes 12582916
  274.8 167.0 %collective-permute-start.5 = (bf16[2048,1024]{0,1:T(8,128)(2,1)S(1)}, bf16[2048,1024]{0,1:T(8,128)(2,1)}, u32[]{:S(2)}, u32[]{:S(2)}) collective-permute-start(bf16[2048,1024]{0,1:T(8,128)(2,1)S(1)} %convolution_convert_fusion.3), channel_id=1, source_target_pairs={{0,1},{1,0},{2,3},{3,2},{4,5},{5,4},{6,7},{7,6},{8,9},{9,8},{10,11... | collective-permute-start | bytes 12582920 | tf_op jit(solution)/shard_map/ppermute | solution.py:43
  275.2 77.1 %slice-start = ((s8[8388608]{0:T(1024)(128)(4,1)}), s8[4194304]{0:T(1024)(128)(4,1)S(1)}, s32[]{:S(2)}) async-start(s8[8388608]{0:T(1024)(128)(4,1)} %bitcast.42), calls=%async_computation.1 | async-start | bytes 8388608
  292.1 60.2 %slice-start.1 = ((s8[8388608]{0:T(1024)(128)(4,1)}), s8[4194304]{0:T(1024)(128)(4,1)S(1)}, s32[]{:S(2)}) async-start(s8[8388608]{0:T(1024)(128)(4,1)} %bitcast.42), calls=%async_computation.2 | async-start | bytes 8388608
  292.1 60.2 %copy-start.19 = (f32[2048]{0:T(1024)S(1)}, f32[2048]{0:T(1024)}, u32[]{:S(2)}) copy-start(f32[2048]{0:T(1024)} %copy-done.18) | copy-start | bytes 24580
  292.1 60.2 %copy-start.21 = (f32[1024]{0:T(1024)S(1)}, f32[1024]{0:T(1024)}, u32[]{:S(2)}) copy-start(f32[1024]{0:T(1024)} %copy-done.20) | copy-start | bytes 12292
  352.3 3.3 copy-start.6
  454.4 3.5 copy-start.1
  454.5 8.5 copy-start.13
  454.5 8.5 copy-start.15
  463.0 14.6 %copy-start.30 = (f32[2047]{0:T(1024)S(1)}, f32[2047]{0:T(1024)}, u32[]{:S(2)}) copy-start(f32[2047]{0:T(1024)} %slice.49) | copy-start | bytes 24568
  477.6 7.7 copy-start
  477.6 7.7 copy-start.31
  485.3 4.3 copy-start.23
  485.3 4.3 copy-start.25
  485.3 4.3 copy-start.27
  504.0 9.6 %copy-start.4 = (bf16[2048,1024]{0,1:T(8,128)(2,1)S(1)}, bf16[2048,1024]{0,1:T(8,128)(2,1)}, u32[]{:S(2)}) copy-start(bf16[2048,1024]{0,1:T(8,128)(2,1)} %copy.42) | copy-start | bytes 12582916
  504.1 9.6 %copy-start.29 = (f32[2048]{0:T(1024)S(1)}, f32[2048]{0:T(1024)}, u32[]{:S(2)}) copy-start(f32[2048]{0:T(1024)} %copy-done.28) | copy-start | bytes 24580
  504.1 9.5 %copy-start.33 = (f32[1024]{0:T(1024)S(1)}, f32[1024]{0:T(1024)}, u32[]{:S(2)}) copy-start(f32[1024]{0:T(1024)} %copy-done.32) | copy-start | bytes 12292
  513.6 4.1 copy-start.8
  517.8 2.4 copy-start.7
  524.6 20.9 %copy-start.5 = (bf16[2048,1024]{0,1:T(8,128)(2,1)S(1)}, bf16[2048,1024]{0,1:T(8,128)(2,1)}, u32[]{:S(2)}) copy-start(bf16[2048,1024]{0,1:T(8,128)(2,1)} %copy.42) | copy-start | bytes 12582916
  852.5 6.9 slice-start.4
  852.5 6.9 slice-start.5
  859.4 4.7 slice-start.2
  859.4 4.7 slice-start.3
  864.1 5.0 copy-start.16
  864.1 8.6 copy-start.17
Sparse Core Ops, SparseCore 0:
  524.8 327.6 all-reduce.7

commit v2 on v1

--- a/solution.py
+++ b/solution.py
@@ -1,11 +1,18 @@
 import jax
 import jax.numpy as jnp
 from jax import lax
+from jax.experimental import pallas as pl
+from jax.experimental.pallas import tpu as pltpu
 from jax.sharding import PartitionSpec as P
 
 EPS = 1e-05
 F32 = jnp.float32
 BF = jnp.bfloat16
+MESH = pl.DeviceIdType.MESH
+TILE_ROWS, TILE_COLS = 1024, 256
+BLOCK = 256
+SLOTS = 10
+VMEM_BYTES = 60 << 20
 
 
 def distances(lengths, count):
@@ -45,6 +52,418 @@
 
 def swap_core(value, count):
     return lax.ppermute(value, "dp", [(i, i ^ 1) for i in range(count)])
+
+
+def swiglu_kernel(h2_ref, gate_ref, up_ref, hid_ref, slope_ref, silu_ref):
+    h2 = h2_ref[...]
+    gate = dot(h2, gate_ref[...], 1, 0)
+    up = dot(h2, up_ref[...], 1, 0)
+    sig = jax.nn.sigmoid(gate)
+    silu = gate * sig
+    hid_ref[...] = (silu * up).astype(BF)
+    slope_ref[...] = (up * sig * (1.0 + gate * (1.0 - sig))).astype(BF)
+    silu_ref[...] = silu.astype(BF)
+
+
+def swiglu(h2, gate_w, up_w):
+    rows, width = h2.shape
+    hidden = gate_w.shape[1]
+    out = jax.ShapeDtypeStruct((rows, hidden), BF)
+    row_spec = pl.BlockSpec((BLOCK, hidden), lambda i: (i, 0))
+    whole = pl.BlockSpec((width, hidden), lambda i: (0, 0), pipeline_mode=pl.Buffered(1))
+    return pl.pallas_call(
+        swiglu_kernel,
+        grid=(rows // BLOCK,),
+        out_shape=(out, out, out),
+        in_specs=[pl.BlockSpec((BLOCK, width), lambda i: (i, 0)), whole, whole],
+        out_specs=(row_spec, row_spec, row_spec),
+        compiler_params=pltpu.CompilerParams(vmem_limit_bytes=VMEM_BYTES),
+    )(h2, gate_w, up_w)
+
+
+class Reducer:
+    def __init__(self, count, tiles, parts, whole, send, recv, out_ref, out_sem):
+        self.count, self.slots = count, tiles.shape[0]
+        self.tiles, self.parts, self.whole = tiles, parts, whole
+        self.send, self.recv = send, recv
+        self.out_ref, self.out_sem = out_ref, out_sem
+        self.me = lax.axis_index("dp")
+        self.side = lax.axis_index("tensor")
+
+    def plan(self, n):
+        me = self.me
+        bit = [me % 2, (me // 2) % 2, (me // 4) % 2, (me // 8) % 2]
+        swap = (n % 4) == 3
+        mine = [bit[0], jnp.where(swap, bit[2], bit[1]), jnp.where(swap, bit[1], bit[2]), bit[3]]
+        step = [1, jnp.where(swap, 4, 2), jnp.where(swap, 2, 4), 8]
+        peer = [me + s * (1 - 2 * b) for s, b in zip(step, mine)]
+        keep, off = [], 0
+        give = []
+        for s in range(4):
+            size = TILE_ROWS >> (s + 1)
+            give.append(pl.multiple_of(off + (1 - mine[s]) * size, size))
+            off = off + mine[s] * size
+            keep.append(pl.multiple_of(off, size))
+        return peer, keep, give
+
+    def scatter(self, n, s):
+        peer, keep, give = self.plan(n)
+        slot = n % self.slots
+        size = TILE_ROWS >> (s + 1)
+        return pltpu.make_async_remote_copy(
+            src_ref=self.tiles.at[slot, pl.ds(give[s], size)],
+            dst_ref=self.parts[s].at[slot],
+            send_sem=self.send.at[slot, s],
+            recv_sem=self.recv.at[slot, s],
+            device_id=(peer[s], self.side),
+            device_id_type=MESH,
+        )
+
+    def gather(self, n, s):
+        peer, keep, give = self.plan(n)
+        slot = n % self.slots
+        size = TILE_ROWS >> (s + 1)
+        block = self.whole.at[slot, pl.ds(keep[s], size)]
+        return pltpu.make_async_remote_copy(
+            src_ref=block,
+            dst_ref=block,
+            send_sem=self.send.at[slot, 4 + s],
+            recv_sem=self.recv.at[slot, 4 + s],
+            device_id=(peer[s], self.side),
+            device_id_type=MESH,
+        )
+
+    def write(self, n):
+        slot = n % self.slots
+        column = pl.multiple_of(n * TILE_COLS, TILE_COLS)
+        return pltpu.make_async_copy(
+            self.whole.at[slot], self.out_ref.at[:, pl.ds(column, TILE_COLS)], self.out_sem.at[slot]
+        )
+
+    def add(self, n, s):
+        peer, keep, give = self.plan(n)
+        slot = n % self.slots
+        size = TILE_ROWS >> (s + 1)
+        rows = pl.ds(keep[s], size)
+        total = self.tiles[slot, rows, :].astype(F32) + self.parts[s][slot].astype(F32)
+        into = self.whole if s == 3 else self.tiles
+        into[slot, rows, :] = total.astype(BF)
+
+    def put(self, n, value):
+        self.tiles[n % self.slots] = value.astype(BF)
+        self.scatter(n, 0).start()
+
+    def tick(self, n):
+        def stage(k):
+            m = n - k
+
+            @pl.when((m >= 0) & (m < self.count))
+            def _():
+                if k <= 4:
+                    self.scatter(m, k - 1).wait()
+                    self.add(m, k - 1)
+                    if k < 4:
+                        self.scatter(m, k).start()
+                    else:
+                        self.gather(m, 3).start()
+                elif k <= 8:
+                    self.gather(m, 8 - k).wait()
+                    if k < 8:
+                        self.gather(m, 7 - k).start()
+                    else:
+                        self.write(m).start()
+                else:
+                    self.write(m).wait()
+
+        for k in (1, 6, 2, 3, 4, 5, 7, 8, 9):
+            stage(k)
+
+
+def ffn_kernel(
+    hid_ref,
+    slope_ref,
+    silu_ref,
+    h2_ref,
+    dy_ref,
+    gate_ref,
+    up_ref,
+    down_ref,
+    sums_ref,
+    dgu_ref,
+    dh2_own_ref,
+    dh2_got_ref,
+    ffn_own_ref,
+    ffn_got_ref,
+    dy_v,
+    h2_v,
+    gate_v,
+    up_v,
+    down_v,
+    tile_v,
+    slope_v,
+    silu_v,
+    dgu_v,
+    row_v,
+    hid_v,
+    tiles,
+    whole,
+    part0,
+    part1,
+    part2,
+    part3,
+    load_sem,
+    tile_sem,
+    pair_sem,
+    dgu_sem,
+    own_sem,
+    hid_sem,
+    x_send,
+    x_recv,
+    send,
+    recv,
+    out_sem,
+):
+    me, side = lax.axis_index("dp"), lax.axis_index("tensor")
+    hidden = hid_ref.shape[1]
+    rows = hid_ref.shape[0]
+    down_tiles = hidden // TILE_COLS
+    count = 3 * down_tiles
+    blocks = rows // BLOCK
+    red = Reducer(count, tiles, (part0, part1, part2, part3), whole, send, recv, sums_ref, out_sem)
+
+    loads = [
+        pltpu.make_async_copy(src, dst, load_sem.at[i])
+        for i, (src, dst) in enumerate(
+            (
+                (dy_ref, dy_v),
+                (down_ref, down_v),
+                (gate_ref, gate_v),
+                (up_ref, up_v),
+                (h2_ref, h2_v),
+            )
+        )
+    ]
+
+    def hid_tile(n):
+        column = pl.multiple_of(n * TILE_COLS, TILE_COLS)
+        return pltpu.make_async_copy(
+            hid_ref.at[:, pl.ds(column, TILE_COLS)], tile_v.at[n % 2], tile_sem.at[n % 2]
+        )
+
+    def dgu_tile(n):
+        column = pl.multiple_of(n * TILE_COLS, TILE_COLS)
+        return pltpu.make_async_copy(
+            dgu_ref.at[:, pl.ds(column, TILE_COLS)], tile_v.at[n % 2], tile_sem.at[n % 2]
+        )
+
+    def block_rows(i):
+        return pl.ds(pl.multiple_of((blocks - 1 - i) * BLOCK, BLOCK), BLOCK)
+
+    def pair(i):
+        at = block_rows(i)
+        return (
+            pltpu.make_async_copy(slope_ref.at[at], slope_v.at[i % 2], pair_sem.at[i % 2, 0]),
+            pltpu.make_async_copy(silu_ref.at[at], silu_v.at[i % 2], pair_sem.at[i % 2, 1]),
+        )
+
+    def dgu_out(i):
+        return pltpu.make_async_copy(dgu_v.at[i % 2], dgu_ref.at[block_rows(i)], dgu_sem.at[i % 2])
+
+    def hid_rows(i):
+        return pltpu.make_async_copy(hid_ref.at[block_rows(i)], hid_v.at[i % 2], hid_sem.at[i % 2])
+
+    def row_own(i, ref):
+        return pltpu.make_async_copy(row_v.at[i % 2], ref.at[block_rows(i % blocks)], own_sem.at[i % 2])
+
+    def row_send(i, ref):
+        return pltpu.make_async_remote_copy(
+            src_ref=row_v.at[i % 2],
+            dst_ref=ref.at[block_rows(i % blocks)],
+            send_sem=x_send.at[i % 2],
+            recv_sem=x_recv.at[i],
+            device_id=(me, 1 - side),
+            device_id_type=MESH,
+        )
+
+    loads[0].start()
+    hid_tile(0).start()
+    for copy in loads[1:]:
+        copy.start()
+    for copy in pair(0):
+        copy.start()
+
+    barrier = pltpu.get_barrier_semaphore()
+    for other in ((1, 2, 4, 8)):
+        pl.semaphore_signal(
+            barrier,
+            inc=1,
+            device_id=(me + other * (1 - 2 * ((me // other) % 2)), side),
+            device_id_type=MESH,
+        )
+    pl.semaphore_signal(barrier, inc=1, device_id=(me, 1 - side), device_id_type=MESH)
+    pl.semaphore_wait(barrier, 5)
+    loads[0].wait()
+
+    def down_step(n, carry):
+        @pl.when(n + 1 < down_tiles)
+        def _():
+            hid_tile(n + 1).start()
+
+        hid_tile(n).wait()
+        red.put(n, dot(dy_v[...], tile_v[n % 2], 0, 0))
+        return carry
+
+    lax.fori_loop(0, 3, down_step, 0)
+    red.tick(1)
+    lax.fori_loop(3, down_tiles, down_step, 0)
+    for copy in loads[1:4]:
+        copy.wait()
+
+    def grad_step(i, carry):
+        slot = i % 2
+
+        @pl.when(i + 1 < blocks)
+        def _():
+            for copy in pair(i + 1):
+                copy.start()
+
+        for copy in pair(i):
+            copy.wait()
+
+        @pl.when(i >= 2)
+        def _():
+            dgu_out(i - 2).wait()
+            row_own(i - 2, dh2_own_ref).wait()
+            row_send(i - 2, dh2_got_ref).wait_send()
+
+        d_hid = dot(dy_v[block_rows(i), :], down_v[...], 1, 1)
+        dgu_v[slot, :, :hidden] = (d_hid * slope_v[slot].astype(F32)).astype(BF)
+        dgu_v[slot, :, hidden:] = (d_hid * silu_v[slot].astype(F32)).astype(BF)
+        dgu_out(i).start()
+        total = dot(dgu_v[slot, :, :hidden], gate_v[...], 1, 1)
+        total = total + dot(dgu_v[slot, :, hidden:], up_v[...], 1, 1)
+        row_v[slot] = total.astype(BF)
+        row_own(i, dh2_own_ref).start()
+        row_send(i, dh2_got_ref).start()
+        red.tick(2 + i)
+        return carry
+
+    lax.fori_loop(0, blocks, grad_step, 0)
+    for i in (blocks - 2, blocks - 1):
+        dgu_out(i).wait()
+    dgu_tile(0).start()
+    hid_rows(0).start()
+    loads[4].wait()
+
+    def pair_tile(k):
+        @pl.when(k + 1 < 2 * down_tiles)
+        def _():
+            dgu_tile(k + 1).start()
+
+        dgu_tile(k).wait()
+        red.put(down_tiles + k, dot(h2_v[...], tile_v[k % 2], 0, 0))
+        red.tick(down_tiles + 1 + k)
+
+    def ffn_step(k, carry):
+        @pl.when(k + 1 < blocks)
+        def _():
+            hid_rows(k + 1).start()
+
+        hid_rows(k).wait()
+        i = blocks + k
+
+        @pl.when(k < 2)
+        def _():
+            row_own(i - 2, dh2_own_ref).wait()
+            row_send(i - 2, dh2_got_ref).wait_send()
+
+        @pl.when(k >= 2)
+        def _():
+            row_own(i - 2, ffn_own_ref).wait()
+            row_send(i - 2, ffn_got_ref).wait_send()
+
+        row_v[k % 2] = dot(hid_v[k % 2], down_v[...], 1, 0).astype(BF)
+        row_own(i, ffn_own_ref).start()
+        row_send(i, ffn_got_ref).start()
+        pair_tile(k)
+        return carry
+
+    lax.fori_loop(0, blocks, ffn_step, 0)
+
+    def tail_step(k, carry):
+        pair_tile(k)
+        return carry
+
+    lax.fori_loop(blocks, 2 * down_tiles, tail_step, 0)
+
+    def drain_step(n, carry):
+        red.tick(n)
+        return carry
+
+    lax.fori_loop(count + 1, count + 10, drain_step, 0)
+    for i in range(blocks):
+        row_send(i, dh2_got_ref).wait_recv()
+    for i in range(blocks, 2 * blocks):
+        row_send(i, ffn_got_ref).wait_recv()
+    for i in (2 * blocks - 2, 2 * blocks - 1):
+        row_own(i, ffn_own_ref).wait()
+        row_send(i, ffn_got_ref).wait_send()
+
+
+def ffn_backward(hid, slope, silu, h2, dy, gate_w, up_w, down_w):
+    rows, hidden = hid.shape
+    width = h2.shape[1]
+    count = 3 * hidden // TILE_COLS
+    blocks = rows // BLOCK
+    any_spec = pl.BlockSpec(memory_space=pl.ANY)
+    dma = pltpu.SemaphoreType.DMA
+    shape = jax.ShapeDtypeStruct
+    return pl.pallas_call(
+        ffn_kernel,
+        out_shape=(
+            shape((TILE_ROWS, count * TILE_COLS), BF),
+            shape((rows, 2 * hidden), BF),
+            shape((rows, width), BF),
+            shape((rows, width), BF),
+            shape((rows, width), BF),
+            shape((rows, width), BF),
+        ),
+        in_specs=[any_spec] * 8,
+        out_specs=(any_spec,) * 6,
+        scratch_shapes=[
+            pltpu.VMEM((rows, width), BF),
+            pltpu.VMEM((rows, width), BF),
+            pltpu.VMEM(gate_w.shape, BF),
+            pltpu.VMEM(up_w.shape, BF),
+            pltpu.VMEM(down_w.shape, BF),
+            pltpu.VMEM((2, rows, TILE_COLS), BF),
+            pltpu.VMEM((2, BLOCK, hidden), BF),
+            pltpu.VMEM((2, BLOCK, hidden), BF),
+            pltpu.VMEM((2, BLOCK, 2 * hidden), BF),
+            pltpu.VMEM((2, BLOCK, width), BF),
+            pltpu.VMEM((2, BLOCK, hidden), BF),
+            pltpu.VMEM((SLOTS, TILE_ROWS, TILE_COLS), BF),
+            pltpu.VMEM((SLOTS, TILE_ROWS, TILE_COLS), BF),
+            pltpu.VMEM((SLOTS, TILE_ROWS // 2, TILE_COLS), BF),
+            pltpu.VMEM((SLOTS, TILE_ROWS // 4, TILE_COLS), BF),
+            pltpu.VMEM((SLOTS, TILE_ROWS // 8, TILE_COLS), BF),
+            pltpu.VMEM((SLOTS, TILE_ROWS // 16, TILE_COLS), BF),
+            dma((5,)),
+            dma((2,)),
+            dma((2, 2)),
+            dma((2,)),
+            dma((2,)),
+            dma((2,)),
+            dma((2,)),
+            dma((2 * blocks,)),
+            dma((SLOTS, 8)),
+            dma((SLOTS, 8)),
+            dma((SLOTS,)),
+        ],
+        compiler_params=pltpu.CompilerParams(
+            collective_id=1, has_side_effects=True, vmem_limit_bytes=VMEM_BYTES
+        ),
+    )(hid, slope, silu, h2, dy, gate_w, up_w, down_w)
 
 
 def fetch_other(weight, core, count):
@@ -112,23 +531,14 @@
     normed2 = resid * scale2
     h2b = (normed2 * g2).astype(BF)
 
-    gate = dot(h2b, gate_weight, 1, 0)
-    up = dot(h2b, up_weight, 1, 0)
-    sig = jax.nn.sigmoid(gate)
-    silu = gate * sig
-    hidb = (silu * up).astype(BF)
-    down_grad = dot(hidb, cotangent, 0, 0).astype(BF)
-    down_sum = lax.psum(down_grad, "dp")
-    d_hid = dot(cotangent, down_weight, 1, 1)
-    d_gate = (d_hid * up * sig * (1.0 + gate * (1.0 - sig))).astype(BF)
-    d_up = (d_hid * silu).astype(BF)
-    dh2_own = (dot(d_gate, gate_weight, 1, 1) + dot(d_up, up_weight, 1, 1)).astype(BF)
-    dh2_got = swap_tensor(dh2_own)
-    gate_grad = dot(h2b, d_gate, 0, 0).astype(BF)
-    up_grad = dot(h2b, d_up, 0, 0).astype(BF)
-    gate_sum, up_sum = lax.psum((gate_grad, up_grad), "dp")
-    ffn_own = dot(hidb, down_weight, 1, 0).astype(BF)
-    ffn_got = swap_tensor(ffn_own)
+    hidb, slope, silu = swiglu(h2b, gate_weight, up_weight)
+    sums, _, dh2_own, dh2_got, ffn_own, ffn_got = ffn_backward(
+        hidb, slope, silu, h2b, cotangent, gate_weight, up_weight, down_weight
+    )
+    hidden = gate_weight.shape[1]
+    down_sum = sums[:, :hidden].T
+    gate_sum = sums[:, hidden : 2 * hidden]
+    up_sum = sums[:, 2 * hidden :]
 
     dh2 = dh2_own.astype(F32) + dh2_got.astype(F32)
     d_resid, g2_grad = norm_back(dh2, normed2, scale2, g2)
@@ -290,7 +700,7 @@
 
 
 def solution(mesh):
-    paired = mesh.shape["tensor"] == 2 and mesh.shape["dp"] % 2 == 0
+    paired = mesh.shape["tensor"] == 2 and mesh.shape["dp"] == 16
     return jax.shard_map(
         pair_body if paired else body,
         mesh=mesh,

time: 890 us -> 703 us (0.79)
  waiting for transfers between devices: 377 us -> 49.1 us
  Pallas kernels: 0 us -> 308 us
  matrix products: 228 us -> 81.8 us
  local copies, waits for them, and re-layouts: 41.7 us -> 23 us
    pallas_call x0 -> x2, Pallas kernels: none -> 308 us  [the longest x1 279 us: ffn_backward(): pl.pallas_call(ffn_kernel, out_shape=(shape((TILE_ROWS, count * TILE_COLS...]
    psum x1, waiting for transfers between devices: 212 us -> 8.34 us  [pair_body(): in_sum, out_sum = lax.psum((in_grad, out_grad), 'dp')]
    dot_general x17 -> x8, matrix products: 228 us -> 81.8 us  [dot(): lax.dot_general(a, b, (((ca,), (cb,)), ((), ())), preferred_element_type=...]
    ppermute x5 -> x3, waiting for transfers between devices: 165 us -> 38.8 us  [swap_tensor(): return lax.ppermute(value, 'tensor', [(0, 1), (1, 0)])]
    unnamed x109 -> x32, local copies, waits for them, and re-layouts: 37.2 us -> 19.7 us
    convert_element_type x2 -> x0, other arithmetic: 11.6 us -> none  [the longest x1 6.93 us: pair_body(): gate_sum.astype(F32)]
    convert_element_type x1, other arithmetic: 4.94 us -> 13.9 us  [pair_body(): down_sum.astype(F32)]
  transfers between devices with their start and end apart: 8 -> 6, of which waited for: 5 -> 4; matrix products, arithmetic and copies ran while one was open for 14% -> 7% of each run, Pallas kernels for 0% -> 0%
where the time goes in v2:
time: 703 us; the launch traced here: 694 us
  Pallas kernels  308 us (44%)
  other arithmetic  151 us (21%)
  matrix products  81.8 us (12%)
  blocking collectives  60.9 us (9%)
  waiting for transfers between devices  49.1 us (7%)
  local copies, waits for them, and re-layouts  23 us (3%)
  between operations  14.8 us (2%)
    pallas_call x1, Pallas kernels, ffn_backward(): pl.pallas_call(ffn_kernel, out_shape=(shape((TILE_ROWS, count * TILE_COLS...  279 us
    dot_general x8, matrix products, dot(): lax.dot_general(a, b, (((ca,), (cb,)), ((), ())), preferred_element_type=...  81.8 us
    psum x1, blocking collectives, pair_body(): g1_sum, conv_sum, g2_sum = lax.psum((g1_grad, conv_grad, g2_grad), 'dp')  60.9 us
    ppermute x3, waiting for transfers between devices, swap_tensor(): return lax.ppermute(value, 'tensor', [(0, 1), (1, 0)])  38.8 us
    pallas_call x1, Pallas kernels, swiglu(): pl.pallas_call(swiglu_kernel, grid=(rows // BLOCK,), out_shape=(out, out,...  29.1 us
    convert_element_type x1, other arithmetic, pair_body(): zb = (c_part * conv_out).astype(BF)  28.1 us
    unnamed x32, local copies, waits for them, and re-layouts  19.7 us
    convert_element_type x1, other arithmetic, pair_body(): d_b = (d_mixed * x_part).astype(BF)  14.4 us
  transfers between devices with their start and end apart: 6, of which 4 were waited for; matrix products, arithmetic and copies ran while one was open for 7% of the time, Pallas kernels for 0%

profile of v2, /device:TPU:0, one launch (start us, length us, event | category | flops | bytes accessed | tf_op | source)
XLA Modules:
  0.0 694.4 jit_solution(11445258196443338616)
XLA Ops:
  7.2 0.0 copy-start.11
  7.2 0.0 copy-start.14
  7.2 0.0 all-reduce.8.cloned.1.call-start
  7.3 3.2 copy.29
  10.5 1.3 constant_dynamic-slice_fusion.1
  11.8 2.9 collective-permute-start
  14.7 0.0 collective-permute-start.2
  14.8 1.9 constant_dynamic-slice_fusion
  16.6 2.0 collective-permute-start.3
  18.6 0.2 reduce-window_clone.1
  18.8 0.1 select_reduce_fusion
  18.9 31.3 %collective-permute-done = bf16[512,1536]{0,1:T(8,128)(2,1)} collective-permute-done((bf16[512,1536]{0,1:T(8,128)(2,1)}, bf16[512,1536]{0,1:T(8,128)(2,1)}, u32[]{:S(2)}, u32[]{:S(2)}) %collective-permute-start) | collective-permute-done | bytes 1572896 | tf_op jit(solution)/shard_map/ppermute | solution.py:50
  50.3 0.0 collective-permute-start.1
  50.3 3.1 fusion.17
  53.4 7.4 %collective-permute-done.3 = bf16[256,1024]{1,0:T(8,128)(2,1)} collective-permute-done((bf16[256,1024]{1,0:T(8,128)(2,1)}, bf16[256,1024]{1,0:T(8,128)(2,1)}, u32[]{:S(2)}, u32[]{:S(2)}) %collective-permute-start.3) | collective-permute-done | bytes 524320 | tf_op jit(solution)/shard_map/ppermute | solution.py:50
  60.8 0.0 collective-permute-start.4
  60.8 0.1 slice.63
  60.9 0.1 slice.61
  61.0 0.0 collective-permute-done.2
  61.0 2.0 collective-permute-done.4
  63.0 1.3 broadcast_select_fusion.7
  64.3 3.1 broadcast_select_fusion.5
  67.4 0.0 collective-permute-done.1
  67.4 2.1 broadcast_select_fusion.3
  69.5 0.4 pad_maximum_fusion.1
  69.9 0.4 broadcast_select_fusion.1
  70.3 0.0 copy-start.4
  70.3 3.4 pad_maximum_fusion
  73.8 18.7 %fusion.64 = f32[2048,3072]{1,0:T(8,128)} fusion(bf16[1024,3072]{0,1:T(8,128)(2,1)} %bitcast.28, bf16[2048,1024]{1,0:T(8,128)(2,1)S(1)} %copy-done.4, f32[1024]{0:T(1024)S(1)} %convert_element_type.93, f32[2048]{0:T(1024)S(1)} %add_rsqrt_fusion.1), kind=kOutput, calls=%fused_computation.104 | convolution fusion | flops 12893290496 | bytes 35663872 | tf_op jit(solution)/shard_map/dot_general | solution.py:46
  92.5 12.0 %slice_multiply_fusion.2 = f32[2048,1024]{1,0:T(8,128)} fusion(f32[2048,3072]{1,0:T(8,128)} %fusion.64), kind=kLoop, calls=%fused_computation.40 | loop fusion | flops 2097152 | bytes 25165824 | tf_op jit(solution)/shard_map/mul | solution.py:524
  104.5 28.1 %multiply_convert_fusion.4 = (bf16[2048,1024]{1,0:T(8,128)(2,1)}, f32[2048,1024]{1,0:T(8,128)}, f32[2048,1024]{1,0:T(8,128)}, f32[2048,1024]{1,0:T(8,128)}) fusion(f32[2048,3072]{1,0:T(8,128)} %fusion.64, f32[1024]{0:T(1024)S(1)} %bitcast.34, f32[1024]{0:T(1024)S(1)} %bitcast.32, f32[1024]{0:T(1024)S(1)} %bitcast.30, f32[2048]{0:T(1024)S(1)} %get-tuple-element.90, ...), kind=kLoop, calls=%fused_computation.35 | loop fusion | flops 20971520 | bytes 71319552 | tf_op jit(solution)/shard_map/convert_element_type | solution.py:528
  132.6 6.6 multiply_reduce_fusion.2
  139.3 3.3 copy-done.2
  142.6 2.4 multiply_convert_fusion.3.h2_ref
  145.0 29.1 %shard_map.186 = (bf16[2048,2304]{1,0:T(8,128)(2,1)}, bf16[2048,2304]{1,0:T(8,128)(2,1)}, bf16[2048,2304]{1,0:T(8,128)(2,1)}) custom-call(bf16[2048,1024]{1,0:T(8,128)(2,1)} %multiply_convert_fusion.3.h2_ref, bf16[1024,2304]{1,0:T(8,128)(2,1)} %gate_ref.3, bf16[1024,2304]{1,0:T(8,128)(2,1)} %up_ref.3), custom_call_target="tpu_custom_call" | custom-call | tf_op jit(solution)/shard_map/pallas_call | solution.py:74
  174.1 279.3 %shard_map.187 = (bf16[1024,6912]{1,0:T(8,128)(2,1)}, bf16[2048,4608]{1,0:T(8,128)(2,1)}, bf16[2048,1024]{1,0:T(8,128)(2,1)}, bf16[2048,1024]{1,0:T(8,128)(2,1)}...) custom-call(bf16[2048,2304]{1,0:T(8,128)(2,1)} %get-tuple-element.18.hid_ref, ...), custom_call_target="tpu_custom_call" | custom-call | tf_op jit(solution)/shard_map/pallas_call | solution.py:421
  453.5 0.0 copy-start.3
  453.5 7.3 %multiply_reduce_fusion = (f32[1024]{0:T(1024)S(1)}, f32[2048]{0:T(1024)S(1)}) fusion(bf16[2048,1024]{1,0:T(8,128)(2,1)} %get-tuple-element.24, bf16[2048,1024]{1,0:T(8,128)(2,1)} %get-tuple-element.23, f32[2048,1024]{1,0:T(8,128)} %copy-done.2, f32[2048]{0:T(1024)S(1)} %add_rsqrt_fusion, f32[1024]{0:T(1024)S(1)} %convert_element_type.99), kind=kLoop, calls=%fused_computation.24 | loop fusion | flops 18871296 | bytes 16801792 | tf_op jit(solution)/shard_map/reduce_sum | solution.py:42
  460.8 0.0 copy-done.3
  460.8 12.5 %multiply_add_fusion.1 = (f32[2048,1024]{1,0:T(8,128)S(1)}, bf16[2048,1024]{1,0:T(8,128)(2,1)}) fusion(bf16[2048,1024]{1,0:T(8,128)(2,1)S(1)} %copy-done.3, bf16[2048,1024]{1,0:T(8,128)(2,1)} %get-tuple-element.24, bf16[2048,1024]{1,0:T(8,128)(2,1)} %get-tuple-element.23, f32[2048,1024]{1,0:T(8,128)} %copy-done.2, f32[2048]{0:T(1024)S(1)} %broadcast_multiply_fusion.1, ...), kind=kLoop, calls=%fused_computation.29 | loop fusion | flops 31457280 | bytes 41963520 | tf_op jit(solution)/shard_map/add | solution.py:545
  473.3 0.0 copy-start.7
  473.3 3.5 copy-done.1
  476.9 4.9 fusion.39
  481.8 0.0 copy-done.7
  481.8 14.4 %multiply_convert_fusion.1 = (bf16[2048,1024]{1,0:T(8,128)(2,1)}, f32[2048,1024]{1,0:T(8,128)}) fusion(f32[2048,1024]{1,0:T(8,128)} %get-tuple-element.71, f32[2048,3072]{1,0:T(8,128)} %fusion.64, bf16[512,1024]{1,0:T(8,128)(2,1)S(1)} %copy-done.9, bf16[512,1024]{1,0:T(8,128)(2,1)S(1)} %copy-done.7, f32[2048,1024]{1,0:T(8,128)} %copy-done.1), kind=kOutput, calls=%fused_computation.26 | convolution fusion | flops 4307550208 | bytes 39845888 | tf_op jit(solution)/shard_map/dot_general | solution.py:46
  496.2 5.5 fusion.47
  501.7 4.3 slice_multiply_fusion
  506.0 4.2 slice_multiply_fusion.1
  510.2 14.4 %multiply_convert_fusion.2 = (bf16[2048,1024]{1,0:T(8,128)(2,1)}, f32[2048,1024]{1,0:T(8,128)}) fusion(f32[2048,3072]{1,0:T(8,128)} %fusion.64, f32[2046,1024]{1,0:T(8,128)} %slice_multiply_fusion, f32[1024]{0:T(1024)S(1)} %bitcast.35, f32[2047,1024]{1,0:T(8,128)} %slice_multiply_fusion.1, f32[1024]{0:T(1024)S(1)} %bitcast.33, f32[2048,1024]{1,0:T(8,128)S(1)} %copy-done, ...), kind=kLoop, calls=%fused_computation.27 | loop fusion | flops 14680064 | bytes 46137344 | tf_op jit(solution)/shard_map/convert_element_type | solution.py:566
  524.6 0.0 copy-start.5
  524.6 9.5 %multiply_convert_fusion = bf16[2048,1024]{1,0:T(8,128)(2,1)} fusion(f32[2048,1024]{1,0:T(8,128)} %get-tuple-element.69, f32[2048,3072]{1,0:T(8,128)} %fusion.64), kind=kLoop, calls=%fused_computation.25 | loop fusion | flops 4194304 | bytes 20971520 | tf_op jit(solution)/shard_map/convert_element_type | solution.py:568
  534.1 5.1 fusion.44
  539.2 21.1 %fusion.16 = (f32[1024]{0:T(1024)S(1)}, f32[2048]{0:T(1024)S(1)}, f32[2048,1024]{1,0:T(8,128)}) fusion(bf16[2048,1024]{1,0:T(8,128)(2,1)} %param.11, f32[2048]{0:T(1024)S(1)} %add_rsqrt_fusion.1, f32[1024]{0:T(1024)S(1)} %convert_element_type.93, bf16[1024,3072]{0,1:T(8,128)(2,1)} %bitcast.29, bf16[2048,1024]{1,0:T(8,128)(2,1)} %multiply_convert_fusion, ...), kind=kOutput, calls=%fused_computation.20 | convolution fusion | flops 12937327616 | bytes 31481856 | tf_op jit(solution)/shard_map/dot_general | solution.py:46
  560.3 5.4 fusion.50
  565.7 2.0 pad_maximum_fusion.2
  567.7 0.0 all-reduce.8.cloned.1.call-update
  567.8 13.9 %convert_bitcast_fusion = (f32[2304,1024]{0,1:T(8,128)}, f32[1024,2304]{1,0:T(8,128)}, f32[1024,2304]{1,0:T(8,128)}) fusion(bf16[1024,6912]{1,0:T(8,128)(2,1)} %get-tuple-element.25), kind=kLoop, calls=%fused_computation.13 | loop fusion | flops 7077888 | bytes 42467328 | tf_op jit(solution)/shard_map/convert_element_type | solution.py:589
  581.6 9.6 %copy.32 = f32[2304,1024]{1,0:T(8,128)} copy(f32[2304,1024]{0,1:T(8,128)} %get-tuple-element.74) | data formatting | bytes 18874368
  591.3 7.8 %multiply_reduce_fusion.5 = (f32[512]{0:T(512)S(1)}, f32[512]{0:T(512)S(1)}, f32[512]{0:T(512)S(1)}) fusion(f32[2048,1024]{1,0:T(8,128)} %slice_multiply_fusion.2, s32[]{:T(128)S(6)} %select_n.106, f32[2048,1024]{1,0:T(8,128)} %get-tuple-element.78, f32[2048,1024]{1,0:T(8,128)} %get-tuple-element.73, f32[2048,1024]{1,0:T(8,128)} %get-tuple-element.72), kind=kLoop, calls=%fused_computation.47 | loop fusion | flops 6289920 | bytes 16783364 | tf_op jit(solution)/shard_map/reduce_sum | solution.py:555
  599.1 60.9 %all-reduce.4 = (f32[1024]{0:T(1024)}, f32[3,512]{1,0:T(4,128)}, f32[1024]{0:T(1024)}) all-reduce(f32[1024]{0:T(1024)S(1)} %get-tuple-element.58, f32[3,512]{1,0:T(4,128)S(1)} %pad_maximum_fusion.7, f32[1024]{0:T(1024)S(1)} %get-tuple-element.56), channel_id=1, replica_groups=mesh['dp'=16,'tensor'=2] {'dp'}, use_global_device_ids=true, to_apply=%region_7.8 | all-reduce | flops 3584 | bytes 28672 | tf_op jit(solution)/shard_map/psum | solution.py:578
  660.0 10.5 %fusion.15 = bf16[2048,1024]{1,0:T(8,128)(2,1)} fusion(f32[2048,1024]{1,0:T(8,128)} %copy-done.1, bf16[2048,1024]{1,0:T(8,128)(2,1)} %param.11, f32[2048,1024]{1,0:T(8,128)} %get-tuple-element.98, f32[2048]{0:T(1024)S(1)} %broadcast_multiply_fusion, f32[1024]{0:T(1024)S(1)} %convert_element_type.93, f32[2048]{0:T(1024)S(1)} %add_rsqrt_fusion.1), kind=kLoop, calls=%fused_computation.19 | loop fusion | flops 16777216 | bytes 25186304 | tf_op jit(solution)/shard_map/convert_element_type | solution.py:575
  670.5 8.3 %all-reduce.8.cloned.1.call-done = (bf16[1024,3,512]{2,0,1:T(8,128)(2,1)}, bf16[512,1024]{1,0:T(8,128)(2,1)}) async-done(((bf16[1024,3,512]{2,0,1:T(8,128)(2,1)}, bf16[512,1024]{1,0:T(8,128)(2,1)}), (bf16[1024,3,512]{2,0,1:T(8,128)(2,1)}, bf16[512,1024]{1,0:T(8,128)(2,1)})) %all-reduce.8.cloned.1.call-update) | async-done | bytes 4194320 | tf_op jit(solution)/shard_map/psum | solution.py:577
  678.8 2.8 convert_element_type.114
  681.6 5.5 convert_element_type.112
  (31 shorter events, 0.1 us)
Async XLA Ops:
  7.2 7.6 %copy-start.11 = (bf16[3,512]{1,0:T(4,128)(2,1)S(1)}, bf16[3,512]{1,0:T(4,128)(2,1)}, u32[]{:S(2)}) copy-start(bf16[3,512]{1,0:T(4,128)(2,1)} %param.16) | copy-start | bytes 9220
  7.2 11.4 %copy-start.14 = (s32[1,3]{1,0:T(1,128)S(1)}, s32[1,3]{1,0:T(1,128)}, u32[]{:S(2)}) copy-start(s32[1,3]{1,0:T(1,128)} %param.13) | copy-start | bytes 40
  7.2 53.6 %copy-start.12 = (bf16[1024]{0:T(1024)(128)(2,1)S(1)}, bf16[1024]{0:T(1024)(128)(2,1)}, u32[]{:S(2)}) copy-start(bf16[1024]{0:T(1024)(128)(2,1)} %param.14) | copy-start | bytes 6148
  7.2 53.6 %copy-start.13 = (bf16[1024]{0:T(1024)(128)(2,1)S(1)}, bf16[1024]{0:T(1024)(128)(2,1)}, u32[]{:S(2)}) copy-start(bf16[1024]{0:T(1024)(128)(2,1)} %param.18) | copy-start | bytes 6148
  7.2 671.6 %all-reduce.8.cloned.1.call-start = ((), (), s32[]{:S(2)}) async-start(), calls=%async_computation | async-start | bytes 8388608 | tf_op jit(solution)/shard_map/psum | solution.py:577
  11.8 38.5 %collective-permute-start = (bf16[512,1536]{0,1:T(8,128)(2,1)}, bf16[512,1536]{0,1:T(8,128)(2,1)}, u32[]{:S(2)}, u32[]{:S(2)}) collective-permute-start(bf16[512,1536]{0,1:T(8,128)(2,1)} %constant_dynamic-slice_fusion.1), channel_id=1, source_target_pairs={{0,1},{1,0},{2,3},{3,2},{4,5},{5,4},{6,7},{7,6},{8,9},{9,8},{10,11... | collective-permute-start | bytes 4718600 | tf_op jit(solution)/shard_map/ppermute | solution.py:50
  14.7 46.2 %collective-permute-start.2 = (bf16[3,512]{1,0:T(4,128)(2,1)S(1)}, bf16[3,512]{1,0:T(4,128)(2,1)S(1)}, u32[]{:S(2)}, u32[]{:S(2)}) collective-permute-start(bf16[3,512]{1,0:T(4,128)(2,1)S(1)} %copy-done.11), channel_id=1, source_target_pairs={{0,1},{1,0},{2,3},{3,2},{4,5},{5,4},{6,7},{7,6},{8,9},{9,8},{10,11... | collective-permute-start | bytes 9224 | tf_op jit(solution)/shard_map/ppermute | solution.py:50
  16.6 44.1 %collective-permute-start.3 = (bf16[256,1024]{1,0:T(8,128)(2,1)}, bf16[256,1024]{1,0:T(8,128)(2,1)}, u32[]{:S(2)}, u32[]{:S(2)}) collective-permute-start(bf16[256,1024]{1,0:T(8,128)(2,1)} %constant_dynamic-slice_fusion), channel_id=1, source_target_pairs={{0,1},{1,0},{2,3},{3,2},{4,5},{5,4},{6,7},{7,6},{8,9},{9,8},{10,11... | collective-permute-start | bytes 1572872 | tf_op jit(solution)/shard_map/ppermute | solution.py:50
  50.3 17.1 %collective-permute-start.1 = (bf16[512,1536]{0,1:T(8,128)(2,1)}, bf16[512,1536]{0,1:T(8,128)(2,1)}, u32[]{:S(2)}, u32[]{:S(2)}) collective-permute-start(bf16[512,1536]{0,1:T(8,128)(2,1)} %collective-permute-done), channel_id=1, source_target_pairs={{0,2},{2,0},{4,6},{6,4},{8,10},{10,8},{12,14},{14,12},{16,18},{18,... | collective-permute-start | bytes 4718600 | tf_op jit(solution)/shard_map/ppermute | solution.py:54
  60.8 2.3 collective-permute-start.4
  70.3 3.5 copy-start.4
  104.5 28.1 %copy-start.6 = (bf16[512,1024]{1,0:T(8,128)(2,1)S(1)}, bf16[512,1024]{1,0:T(8,128)(2,1)}, u32[]{:S(2)}) copy-start(bf16[512,1024]{1,0:T(8,128)(2,1)} %get-tuple-element.85) | copy-start | bytes 3145732
  104.5 28.1 %copy-start.8 = (bf16[512,1024]{1,0:T(8,128)(2,1)S(1)}, bf16[512,1024]{1,0:T(8,128)(2,1)}, u32[]{:S(2)}) copy-start(bf16[512,1024]{1,0:T(8,128)(2,1)} %get-tuple-element.86) | copy-start | bytes 3145732
  139.3 3.3 copy-start.2
  453.5 7.4 %copy-start.3 = (bf16[2048,1024]{1,0:T(8,128)(2,1)S(1)}, bf16[2048,1024]{1,0:T(8,128)(2,1)}, u32[]{:S(2)}) copy-start(bf16[2048,1024]{1,0:T(8,128)(2,1)} %dy_ref.1) | copy-start | bytes 12582916
  473.3 3.5 copy-start.1
  473.3 8.4 %copy-start.7 = (bf16[512,1024]{1,0:T(8,128)(2,1)S(1)}, bf16[512,1024]{1,0:T(8,128)(2,1)}, u32[]{:S(2)}) copy-start(bf16[512,1024]{1,0:T(8,128)(2,1)} %get-tuple-element.85) | copy-start | bytes 3145732
  473.3 8.4 %copy-start.9 = (bf16[512,1024]{1,0:T(8,128)(2,1)S(1)}, bf16[512,1024]{1,0:T(8,128)(2,1)}, u32[]{:S(2)}) copy-start(bf16[512,1024]{1,0:T(8,128)(2,1)} %get-tuple-element.86) | copy-start | bytes 3145732
  496.2 5.5 copy-start
  524.6 9.5 %copy-start.5 = (bf16[2048,1024]{1,0:T(8,128)(2,1)S(1)}, bf16[2048,1024]{1,0:T(8,128)(2,1)}, u32[]{:S(2)}) copy-start(bf16[2048,1024]{1,0:T(8,128)(2,1)} %param.11) | copy-start | bytes 12582916
  560.3 5.5 copy-start.10
Sparse Core Ops, SparseCore 0:
  567.9 110.9 all-reduce.7

commit v3 on v2

--- a/solution.py
+++ b/solution.py
@@ -12,7 +12,7 @@
 TILE_ROWS, TILE_COLS = 1024, 256
 BLOCK = 256
 SLOTS = 10
-VMEM_BYTES = 60 << 20
+VMEM_BYTES = 63 << 20
 
 
 def distances(lengths, count):
@@ -52,6 +52,98 @@
 
 def swap_core(value, count):
     return lax.ppermute(value, "dp", [(i, i ^ 1) for i in range(count)])
+
+
+def block_keeps(lengths_ref, first, count):
+    place = first + lax.broadcasted_iota(jnp.int32, (count, 1), 0)
+    one = place != 0
+    two = (place != 0) & (place != 1)
+    start = 0
+    for j in range(lengths_ref.shape[1] - 1):
+        start = start + lengths_ref[0, j]
+        one = one & (place != start)
+        two = two & (place != start) & (place != start + 1)
+    return one, two
+
+
+def mixer_kernel(
+    lengths_ref,
+    x_ref,
+    gain1_ref,
+    in_ref,
+    taps_ref,
+    out_ref,
+    gain2_ref,
+    h1_ref,
+    keep_ref,
+    z_ref,
+    resid_ref,
+    h2_ref,
+    last,
+):
+    i = pl.program_id(0)
+    count, width = x_ref.shape
+
+    @pl.when(i == 0)
+    def _():
+        last[...] = jnp.zeros_like(last)
+
+    x = x_ref[...].astype(F32)
+    h1 = (x * rms_scale(x) * gain1_ref[...].astype(F32)).astype(BF)
+    h1_ref[...] = h1
+    b_part = dot(h1, in_ref[:, :width], 1, 0)
+    x_part = dot(h1, in_ref[:, 2 * width :], 1, 0)
+    keep_ref[:, :width] = b_part.astype(BF)
+    keep_ref[:, 2 * width : 3 * width] = x_part.astype(BF)
+    m = b_part * x_part
+    one, two = block_keeps(lengths_ref, i * count, count)
+    row = lax.broadcasted_iota(jnp.int32, (count, 1), 0)
+    m_one = jnp.where(row == 0, last[7:8, :], pltpu.roll(m, 1, 0))
+    m_two = jnp.where(row == 0, last[6:7, :], jnp.where(row == 1, last[7:8, :], pltpu.roll(m, 2, 0)))
+    last[...] = m[count - 8 :, :]
+    taps = taps_ref[...].astype(F32)
+    v = taps[0:1] * m + taps[1:2] * jnp.where(one, m_one, 0.0) + taps[2:3] * jnp.where(two, m_two, 0.0)
+    keep_ref[:, 3 * width :] = v.astype(BF)
+    c_part = dot(h1, in_ref[:, width : 2 * width], 1, 0)
+    keep_ref[:, width : 2 * width] = c_part.astype(BF)
+    z = (c_part * v).astype(BF)
+    z_ref[...] = z
+    resid = x + dot(z, out_ref[...], 1, 0)
+    resid_ref[...] = resid
+    h2_ref[...] = (resid * rms_scale(resid) * gain2_ref[...].astype(F32)).astype(BF)
+
+
+def mixer_forward(lengths, x, gain1, in_full, taps, out_full, gain2):
+    rows, width = x.shape
+    block = pl.BlockSpec((BLOCK, width), lambda i: (i, 0))
+
+    def whole(shape):
+        return pl.BlockSpec(shape, lambda i: (0, 0), pipeline_mode=pl.Buffered(1))
+
+    low = jax.ShapeDtypeStruct((rows, width), BF)
+    return pl.pallas_call(
+        mixer_kernel,
+        grid=(rows // BLOCK,),
+        out_shape=(
+            low,
+            jax.ShapeDtypeStruct((rows, 4 * width), BF),
+            low,
+            jax.ShapeDtypeStruct((rows, width), F32),
+            low,
+        ),
+        in_specs=[
+            pl.BlockSpec(memory_space=pltpu.SMEM),
+            block,
+            whole((1, width)),
+            whole(in_full.shape),
+            whole(taps.shape),
+            whole(out_full.shape),
+            whole((1, width)),
+        ],
+        out_specs=(block, pl.BlockSpec((BLOCK, 4 * width), lambda i: (i, 0)), block, block, block),
+        scratch_shapes=[pltpu.VMEM((8, width), F32)],
+        compiler_params=pltpu.CompilerParams(vmem_limit_bytes=VMEM_BYTES),
+    )(lengths, x, gain1.reshape(1, width), in_full, taps, out_full, gain2.reshape(1, width))
 
 
 def swiglu_kernel(h2_ref, gate_ref, up_ref, hid_ref, slope_ref, silu_ref):
@@ -179,7 +271,8 @@
             stage(k)
 
 
-def ffn_kernel(
+def back_kernel(
+    lengths_ref,
     hid_ref,
     slope_ref,
     silu_ref,
@@ -188,23 +281,35 @@
     gate_ref,
     up_ref,
     down_ref,
+    resid_ref,
+    x_ref,
+    keep_ref,
+    z_ref,
+    h1_ref,
+    in_ref,
+    out_ref,
+    gain1_ref,
+    gain2_ref,
+    taps_ref,
     sums_ref,
     dgu_ref,
     dh2_own_ref,
     dh2_got_ref,
     ffn_own_ref,
     ffn_got_ref,
+    dp_ref,
+    grad_ref,
+    result_ref,
+    small_ref,
     dy_v,
     h2_v,
-    gate_v,
-    up_v,
+    wide_v,
     down_v,
     tile_v,
-    slope_v,
-    silu_v,
-    dgu_v,
     row_v,
-    hid_v,
+    small_v,
+    small_in,
+    next_v,
     tiles,
     whole,
     part0,
@@ -213,10 +318,14 @@
     part3,
     load_sem,
     tile_sem,
-    pair_sem,
+    stream_sem,
     dgu_sem,
     own_sem,
     hid_sem,
+    dp_sem,
+    grad_sem,
+    small_send,
+    small_recv,
     x_send,
     x_recv,
     send,
@@ -224,88 +333,102 @@
     out_sem,
 ):
     me, side = lax.axis_index("dp"), lax.axis_index("tensor")
+    rows, width = dy_v.shape
     hidden = hid_ref.shape[1]
-    rows = hid_ref.shape[0]
-    down_tiles = hidden // TILE_COLS
-    count = 3 * down_tiles
+    half = width // 2
     blocks = rows // BLOCK
+    n_down = hidden // TILE_COLS
+    n_out = half // TILE_COLS
+    first_gate, first_out = n_down, 3 * n_down
+    first_in = first_out + n_out
+    count = first_in + 3 * n_out
     red = Reducer(count, tiles, (part0, part1, part2, part3), whole, send, recv, sums_ref, out_sem)
 
-    loads = [
-        pltpu.make_async_copy(src, dst, load_sem.at[i])
-        for i, (src, dst) in enumerate(
-            (
-                (dy_ref, dy_v),
-                (down_ref, down_v),
-                (gate_ref, gate_v),
-                (up_ref, up_v),
-                (h2_ref, h2_v),
-            )
-        )
-    ]
-
-    def hid_tile(n):
-        column = pl.multiple_of(n * TILE_COLS, TILE_COLS)
-        return pltpu.make_async_copy(
-            hid_ref.at[:, pl.ds(column, TILE_COLS)], tile_v.at[n % 2], tile_sem.at[n % 2]
-        )
-
-    def dgu_tile(n):
-        column = pl.multiple_of(n * TILE_COLS, TILE_COLS)
-        return pltpu.make_async_copy(
-            dgu_ref.at[:, pl.ds(column, TILE_COLS)], tile_v.at[n % 2], tile_sem.at[n % 2]
-        )
+    def peer(bit):
+        return me + bit * (1 - 2 * ((me // bit) % 2))
 
     def block_rows(i):
         return pl.ds(pl.multiple_of((blocks - 1 - i) * BLOCK, BLOCK), BLOCK)
 
-    def pair(i):
-        at = block_rows(i)
-        return (
-            pltpu.make_async_copy(slope_ref.at[at], slope_v.at[i % 2], pair_sem.at[i % 2, 0]),
-            pltpu.make_async_copy(silu_ref.at[at], silu_v.at[i % 2], pair_sem.at[i % 2, 1]),
+    load_dy = pltpu.make_async_copy(dy_ref, dy_v, load_sem.at[0])
+    load_down = pltpu.make_async_copy(down_ref, down_v, load_sem.at[1])
+    load_gate = pltpu.make_async_copy(gate_ref, wide_v.at[:, pl.ds(0, hidden)], load_sem.at[2])
+    load_up = pltpu.make_async_copy(up_ref, wide_v.at[:, pl.ds(hidden, hidden)], load_sem.at[3])
+    load_h2 = pltpu.make_async_copy(h2_ref, h2_v, load_sem.at[4])
+    load_in = pltpu.make_async_copy(in_ref, wide_v.at[:, pl.ds(0, 3 * width)], load_sem.at[2])
+    load_out = pltpu.make_async_copy(out_ref, wide_v.at[:, pl.ds(3 * width, width)], load_sem.at[3])
+    load_h1 = pltpu.make_async_copy(h1_ref, h2_v, load_sem.at[4])
+
+    def tile_of(ref, column, n):
+        column = pl.multiple_of(column, TILE_COLS)
+        return pltpu.make_async_copy(
+            ref.at[:, pl.ds(column, TILE_COLS)], tile_v.at[n % 2], tile_sem.at[n % 2]
         )
 
-    def dgu_out(i):
-        return pltpu.make_async_copy(dgu_v.at[i % 2], dgu_ref.at[block_rows(i)], dgu_sem.at[i % 2])
-
-    def hid_rows(i):
-        return pltpu.make_async_copy(hid_ref.at[block_rows(i)], hid_v.at[i % 2], hid_sem.at[i % 2])
+    def hid_tile(n):
+        return tile_of(hid_ref, n * TILE_COLS, n)
+
+    def dgu_tile(n):
+        return tile_of(dgu_ref, (n - first_gate) * TILE_COLS, n)
+
+    def z_tile(n):
+        return tile_of(z_ref, side * half + (n - first_out) * TILE_COLS, n)
+
+    def dp_tile(n):
+        return tile_of(dp_ref, (n - first_in) * TILE_COLS, n)
 
     def row_own(i, ref):
         return pltpu.make_async_copy(row_v.at[i % 2], ref.at[block_rows(i % blocks)], own_sem.at[i % 2])
 
-    def row_send(i, ref):
+    def row_send(i, own, got):
+        at = block_rows(i % blocks)
         return pltpu.make_async_remote_copy(
-            src_ref=row_v.at[i % 2],
-            dst_ref=ref.at[block_rows(i % blocks)],
-            send_sem=x_send.at[i % 2],
+            src_ref=own.at[at],
+            dst_ref=got.at[at],
+            send_sem=x_send.at[i],
             recv_sem=x_recv.at[i],
             device_id=(me, 1 - side),
             device_id_type=MESH,
         )
 
-    loads[0].start()
-    hid_tile(0).start()
-    for copy in loads[1:]:
-        copy.start()
-    for copy in pair(0):
-        copy.start()
-
-    barrier = pltpu.get_barrier_semaphore()
-    for other in ((1, 2, 4, 8)):
-        pl.semaphore_signal(
-            barrier,
-            inc=1,
-            device_id=(me + other * (1 - 2 * ((me // other) % 2)), side),
+    def dh2_send(i):
+        return row_send(i, dh2_own_ref, dh2_got_ref)
+
+    def ffn_send(i):
+        return row_send(blocks + i, ffn_own_ref, ffn_got_ref)
+
+    def small_copy(s):
+        return pltpu.make_async_remote_copy(
+            src_ref=small_v,
+            dst_ref=small_in.at[s],
+            send_sem=small_send.at[s],
+            recv_sem=small_recv.at[s],
+            device_id=(peer(1 << s), side),
             device_id_type=MESH,
         )
+
+    def small_add(s):
+        small_copy(s).wait()
+        small_v[...] = small_v[...] + small_in[s]
+
+    load_dy.start()
+    hid_tile(0).start()
+    load_down.start()
+    load_gate.start()
+    load_up.start()
+    load_h2.start()
+
+    barrier = pltpu.get_barrier_semaphore()
+    for bit in (1, 2, 4, 8):
+        pl.semaphore_signal(barrier, inc=1, device_id=(peer(bit), side), device_id_type=MESH)
     pl.semaphore_signal(barrier, inc=1, device_id=(me, 1 - side), device_id_type=MESH)
     pl.semaphore_wait(barrier, 5)
-    loads[0].wait()
+
+    small_v[...] = jnp.zeros_like(small_v)
+    next_v[...] = jnp.zeros_like(next_v)
 
     def down_step(n, carry):
-        @pl.when(n + 1 < down_tiles)
+        @pl.when(n + 1 < n_down)
         def _():
             hid_tile(n + 1).start()
 
@@ -313,148 +436,365 @@
         red.put(n, dot(dy_v[...], tile_v[n % 2], 0, 0))
         return carry
 
-    lax.fori_loop(0, 3, down_step, 0)
-    red.tick(1)
-    lax.fori_loop(3, down_tiles, down_step, 0)
-    for copy in loads[1:4]:
-        copy.wait()
-
-    def grad_step(i, carry):
-        slot = i % 2
-
-        @pl.when(i + 1 < blocks)
-        def _():
-            for copy in pair(i + 1):
+    def grads(slope_v, silu_v, dgu_v):
+        def pair(i):
+            at = block_rows(i)
+            return (
+                pltpu.make_async_copy(slope_ref.at[at], slope_v.at[i % 2], stream_sem.at[i % 2, 0]),
+                pltpu.make_async_copy(silu_ref.at[at], silu_v.at[i % 2], stream_sem.at[i % 2, 1]),
+            )
+
+        def dgu_out(i):
+            return pltpu.make_async_copy(
+                dgu_v.at[i % 2], dgu_ref.at[block_rows(i)], dgu_sem.at[i % 2]
+            )
+
+        for copy in pair(0):
+            copy.start()
+        load_dy.wait()
+        lax.fori_loop(0, 3, down_step, 0)
+        red.tick(1)
+        lax.fori_loop(3, n_down, down_step, 0)
+        load_down.wait()
+        load_gate.wait()
+        load_up.wait()
+
+        def grad_step(i, carry):
+            slot = i % 2
+
+            @pl.when(i + 1 < blocks)
+            def _():
+                for copy in pair(i + 1):
+                    copy.start()
+
+            for copy in pair(i):
+                copy.wait()
+
+            @pl.when(i >= 2)
+            def _():
+                dgu_out(i - 2).wait()
+
+            d_hid = dot(dy_v[block_rows(i), :], down_v[...], 1, 1)
+            dgu_v[slot, :, :hidden] = (d_hid * slope_v[slot].astype(F32)).astype(BF)
+            dgu_v[slot, :, hidden:] = (d_hid * silu_v[slot].astype(F32)).astype(BF)
+            dgu_out(i).start()
+            row_v[slot] = dot(dgu_v[slot], wide_v[...], 1, 1).astype(BF)
+            row_own(i, dh2_own_ref).start()
+            red.tick(2 + i)
+            row_own(i, dh2_own_ref).wait()
+            dh2_send(i).start()
+            return carry
+
+        lax.fori_loop(0, blocks, grad_step, 0)
+        load_in.start()
+        load_out.start()
+        for i in (blocks - 2, blocks - 1):
+            dgu_out(i).wait()
+        dgu_tile(first_gate).start()
+
+    pl.run_scoped(
+        grads,
+        pltpu.VMEM((2, BLOCK, hidden), BF),
+        pltpu.VMEM((2, BLOCK, hidden), BF),
+        pltpu.VMEM((2, BLOCK, 2 * hidden), BF),
+    )
+
+    def gate_put(n):
+        dgu_tile(n).wait()
+        red.put(n, dot(h2_v[...], tile_v[n % 2], 0, 0))
+
+    def mixer(keep_v, resid_v, x_v, pair_v, hid_v, dp_v, grad_v):
+        def hid_rows(i):
+            return pltpu.make_async_copy(hid_ref.at[block_rows(i)], hid_v.at[i % 2], hid_sem.at[i % 2])
+
+        def inputs(i):
+            at, slot = block_rows(i), i % 2
+            return (
+                pltpu.make_async_copy(keep_ref.at[at], keep_v.at[slot], stream_sem.at[slot, 0]),
+                pltpu.make_async_copy(resid_ref.at[at], resid_v.at[slot], stream_sem.at[slot, 1]),
+                pltpu.make_async_copy(x_ref.at[at], x_v.at[slot], stream_sem.at[slot, 2]),
+                pltpu.make_async_copy(dh2_own_ref.at[at], pair_v.at[0], stream_sem.at[slot, 3]),
+            )
+
+        def got(i):
+            return pltpu.make_async_copy(dh2_got_ref.at[block_rows(i)], pair_v.at[1], dgu_sem.at[0])
+
+        def dp_out(i):
+            at = block_rows(i)
+            return [
+                pltpu.make_async_copy(
+                    dp_v.at[:, pl.ds(pl.multiple_of(k * width + side * half, half), half)],
+                    dp_ref.at[at, pl.ds(k * half, half)],
+                    dp_sem.at[k],
+                )
+                for k in range(3)
+            ]
+
+        def grad_out(i):
+            return pltpu.make_async_copy(grad_v, grad_ref.at[block_rows(i)], grad_sem)
+
+        def finish(i):
+            for copy in dp_out(i):
+                copy.wait()
+            grad_out(i).wait()
+
+        def mixer_block(i):
+            slot = i % 2
+            at = block_rows(i)
+            for copy in inputs(i):
+                copy.wait()
+            got(i).wait()
+
+            @pl.when(i > 0)
+            def _():
+                finish(i - 1)
+
+            resid = resid_v[slot]
+            scale2 = rms_scale(resid)
+            n2 = resid * scale2
+            dh2 = pair_v[0].astype(F32) + pair_v[1].astype(F32)
+            d_resid, gain2_part = norm_back(dh2, n2, scale2, gain2_ref[...].astype(F32))
+            dr1 = dy_v[at, :].astype(F32) + d_resid
+            dr1b = dr1.astype(BF)
+            dy_v[at, :] = dr1b
+            dz = dot(dr1b, wide_v[:, 3 * width : 4 * width], 1, 1)
+            dc = dz * keep_v[slot, :, 3 * width :].astype(F32)
+            dp_v[:, width : 2 * width] = dc.astype(BF)
+            dv = dz * keep_v[slot, :, width : 2 * width].astype(F32)
+            b_part = keep_v[slot, :, :width].astype(F32)
+            x_part = keep_v[slot, :, 2 * width : 3 * width].astype(F32)
+            m = b_part * x_part
+            one, two = block_keeps(lengths_ref, (blocks - 1 - i) * BLOCK, BLOCK)
+            row = lax.broadcasted_iota(jnp.int32, (BLOCK, 1), 0)
+            dv_one = jnp.where(one, dv, 0.0)
+            dv_two = jnp.where(two, dv, 0.0)
+            up_one = jnp.where(row == BLOCK - 1, next_v[0:1, :], pltpu.roll(dv_one, BLOCK - 1, 0))
+            up_two = jnp.where(
+                row == BLOCK - 2,
+                next_v[8:9, :],
+                jnp.where(row == BLOCK - 1, next_v[9:10, :], pltpu.roll(dv_two, BLOCK - 2, 0)),
+            )
+            next_v[0:8, :] = dv_one[0:8]
+            next_v[8:16, :] = dv_two[0:8]
+            taps = taps_ref[...].astype(F32)
+            dm = taps[0:1] * dv + taps[1:2] * up_one + taps[2:3] * up_two
+            dp_v[:, :width] = (dm * x_part).astype(BF)
+            dp_v[:, 2 * width :] = (dm * b_part).astype(BF)
+            for copy in dp_out(i):
                 copy.start()
-
-        for copy in pair(i):
-            copy.wait()
-
-        @pl.when(i >= 2)
-        def _():
-            dgu_out(i - 2).wait()
-            row_own(i - 2, dh2_own_ref).wait()
-            row_send(i - 2, dh2_got_ref).wait_send()
-
-        d_hid = dot(dy_v[block_rows(i), :], down_v[...], 1, 1)
-        dgu_v[slot, :, :hidden] = (d_hid * slope_v[slot].astype(F32)).astype(BF)
-        dgu_v[slot, :, hidden:] = (d_hid * silu_v[slot].astype(F32)).astype(BF)
-        dgu_out(i).start()
-        total = dot(dgu_v[slot, :, :hidden], gate_v[...], 1, 1)
-        total = total + dot(dgu_v[slot, :, hidden:], up_v[...], 1, 1)
-        row_v[slot] = total.astype(BF)
-        row_own(i, dh2_own_ref).start()
-        row_send(i, dh2_got_ref).start()
-        red.tick(2 + i)
-        return carry
-
-    lax.fori_loop(0, blocks, grad_step, 0)
-    for i in (blocks - 2, blocks - 1):
-        dgu_out(i).wait()
-    dgu_tile(0).start()
-    hid_rows(0).start()
-    loads[4].wait()
-
-    def pair_tile(k):
-        @pl.when(k + 1 < 2 * down_tiles)
-        def _():
-            dgu_tile(k + 1).start()
-
-        dgu_tile(k).wait()
-        red.put(down_tiles + k, dot(h2_v[...], tile_v[k % 2], 0, 0))
-        red.tick(down_tiles + 1 + k)
-
-    def ffn_step(k, carry):
-        @pl.when(k + 1 < blocks)
-        def _():
-            hid_rows(k + 1).start()
-
-        hid_rows(k).wait()
-        i = blocks + k
-
-        @pl.when(k < 2)
-        def _():
-            row_own(i - 2, dh2_own_ref).wait()
-            row_send(i - 2, dh2_got_ref).wait_send()
-
-        @pl.when(k >= 2)
-        def _():
-            row_own(i - 2, ffn_own_ref).wait()
-            row_send(i - 2, ffn_got_ref).wait_send()
-
-        row_v[k % 2] = dot(hid_v[k % 2], down_v[...], 1, 0).astype(BF)
-        row_own(i, ffn_own_ref).start()
-        row_send(i, ffn_got_ref).start()
-        pair_tile(k)
-        return carry
-
-    lax.fori_loop(0, blocks, ffn_step, 0)
-
-    def tail_step(k, carry):
-        pair_tile(k)
-        return carry
-
-    lax.fori_loop(blocks, 2 * down_tiles, tail_step, 0)
-
-    def drain_step(n, carry):
-        red.tick(n)
-        return carry
-
-    lax.fori_loop(count + 1, count + 10, drain_step, 0)
-    for i in range(blocks):
-        row_send(i, dh2_got_ref).wait_recv()
-    for i in range(blocks, 2 * blocks):
-        row_send(i, ffn_got_ref).wait_recv()
-    for i in (2 * blocks - 2, 2 * blocks - 1):
-        row_own(i, ffn_own_ref).wait()
-        row_send(i, ffn_got_ref).wait_send()
-
-
-def ffn_backward(hid, slope, silu, h2, dy, gate_w, up_w, down_w):
+            dh1 = dot(dp_v[...], wide_v[:, : 3 * width], 1, 1)
+            x = x_v[slot].astype(F32)
+            scale1 = rms_scale(x)
+            d_input, gain1_part = norm_back(dh1, x * scale1, scale1, gain1_ref[...].astype(F32))
+            grad_v[...] = (dr1 + d_input).astype(BF)
+            grad_out(i).start()
+            small_v[0:1, :] += gain1_part.reshape(1, width)
+            small_v[1:2, :] += gain2_part.reshape(1, width)
+            small_v[2:3, :] += jnp.sum(dv * m, axis=0, keepdims=True)
+            small_v[3:4, :] += jnp.sum(up_one * m, axis=0, keepdims=True)
+            small_v[4:5, :] += jnp.sum(up_two * m, axis=0, keepdims=True)
+
+        hid_rows(0).start()
+        for copy in inputs(0):
+            copy.start()
+        load_h2.wait()
+        load_in.wait()
+        load_out.wait()
+
+        def mixer_step(i, carry):
+            n = first_gate + 2 * i
+            dh2_send(i).wait_recv()
+            got(i).start()
+            dgu_tile(n + 1).start()
+            gate_put(n)
+            red.tick(n + 1)
+            mixer_block(i)
+
+            @pl.when(i + 1 < blocks)
+            def _():
+                hid_rows(i + 1).start()
+                for copy in inputs(i + 1):
+                    copy.start()
+
+            hid_rows(i).wait()
+            row_v[i % 2] = dot(hid_v[i % 2], down_v[...], 1, 0).astype(BF)
+            row_own(i, ffn_own_ref).start()
+            dgu_tile(n + 2).start()
+            gate_put(n + 1)
+            row_own(i, ffn_own_ref).wait()
+            ffn_send(i).start()
+            red.tick(n + 2)
+            return carry
+
+        lax.fori_loop(0, blocks, mixer_step, 0)
+        finish(blocks - 1)
+
+    pl.run_scoped(
+        mixer,
+        pltpu.VMEM((2, BLOCK, 4 * width), BF),
+        pltpu.VMEM((2, BLOCK, width), F32),
+        pltpu.VMEM((2, BLOCK, width), BF),
+        pltpu.VMEM((2, BLOCK, width), BF),
+        pltpu.VMEM((2, BLOCK, hidden), BF),
+        pltpu.VMEM((BLOCK, 3 * width), BF),
+        pltpu.VMEM((BLOCK, width), BF),
+    )
+
+    small_copy(0).start()
+
+    def tail(resid_v, pair_v, result_v):
+        def inputs(i):
+            at = block_rows(i)
+            return (
+                pltpu.make_async_copy(resid_ref.at[at], resid_v, stream_sem.at[0, 0]),
+                pltpu.make_async_copy(ffn_own_ref.at[at], pair_v.at[0], stream_sem.at[0, 1]),
+                pltpu.make_async_copy(ffn_got_ref.at[at], pair_v.at[1], stream_sem.at[0, 2]),
+            )
+
+        def result_out(i):
+            return pltpu.make_async_copy(result_v, result_ref.at[block_rows(i)], grad_sem)
+
+        def post(p):
+            i = p // 2
+
+            @pl.when((p % 2 == 0) & (i < blocks))
+            def _():
+                ffn_send(i).wait_recv()
+                for copy in inputs(i):
+                    copy.start()
+
+            @pl.when((p % 2 == 1) & (i < blocks))
+            def _():
+                for copy in inputs(i):
+                    copy.wait()
+
+                @pl.when(i > 0)
+                def _():
+                    result_out(i - 1).wait()
+
+                both = pair_v[0].astype(F32) + pair_v[1].astype(F32)
+                result_v[...] = (resid_v[...] + both).astype(BF)
+                result_out(i).start()
+
+        base = first_gate + 2 * blocks
+
+        def step(n, put):
+            put(n)
+            red.tick(n + 1)
+            post(n - base)
+
+        for n in range(base, first_out):
+            (dgu_tile if n + 1 < first_out else z_tile)(n + 1).start()
+            step(n, gate_put)
+        load_h1.start()
+        small_add(0)
+        small_copy(1).start()
+
+        def out_put(n):
+            z_tile(n).wait()
+            red.put(n, dot(dy_v[...], tile_v[n % 2], 0, 0))
+
+        for n in range(first_out, first_in):
+            (z_tile if n + 1 < first_in else dp_tile)(n + 1).start()
+            step(n, out_put)
+        small_add(1)
+        small_copy(2).start()
+        load_h1.wait()
+
+        def in_step(n, carry):
+            @pl.when(n + 1 < count)
+            def _():
+                dp_tile(n + 1).start()
+
+            def in_put(n):
+                dp_tile(n).wait()
+                red.put(n, dot(h2_v[...], tile_v[n % 2], 0, 0))
+
+            step(n, in_put)
+            return carry
+
+        middle = (first_in + count) // 2
+        lax.fori_loop(first_in, middle, in_step, 0)
+        small_add(2)
+        small_copy(3).start()
+        lax.fori_loop(middle, count, in_step, 0)
+        small_add(3)
+        small_out = pltpu.make_async_copy(small_v, small_ref, load_sem.at[0])
+        small_out.start()
+
+        def drain_step(n, carry):
+            red.tick(n + 1)
+            post(n - base)
+            return carry
+
+        lax.fori_loop(count, count + 9, drain_step, 0)
+        result_out(blocks - 1).wait()
+        small_out.wait()
+        for i in range(blocks):
+            dh2_send(i).wait_send()
+            ffn_send(i).wait_send()
+
+    pl.run_scoped(
+        tail,
+        pltpu.VMEM((BLOCK, width), F32),
+        pltpu.VMEM((2, BLOCK, width), BF),
+        pltpu.VMEM((BLOCK, width), BF),
+    )
+
+
+def block_backward(
+    lengths, hid, slope, silu, h2, dy, gate_w, up_w, down_w, resid, x, keep, z, h1, in_full, out_full,
+    gain1, gain2, taps,
+):
     rows, hidden = hid.shape
     width = h2.shape[1]
-    count = 3 * hidden // TILE_COLS
+    count = (3 * hidden + 2 * width) // TILE_COLS
     blocks = rows // BLOCK
     any_spec = pl.BlockSpec(memory_space=pl.ANY)
+    vmem_spec = pl.BlockSpec(memory_space=pltpu.VMEM)
     dma = pltpu.SemaphoreType.DMA
     shape = jax.ShapeDtypeStruct
+    low = shape((rows, width), BF)
+    ring = [pltpu.VMEM((SLOTS, TILE_ROWS, TILE_COLS), BF)]
+    ring += [pltpu.VMEM((SLOTS, TILE_ROWS >> s, TILE_COLS), BF) for s in range(5)]
     return pl.pallas_call(
-        ffn_kernel,
+        back_kernel,
         out_shape=(
             shape((TILE_ROWS, count * TILE_COLS), BF),
             shape((rows, 2 * hidden), BF),
-            shape((rows, width), BF),
-            shape((rows, width), BF),
-            shape((rows, width), BF),
-            shape((rows, width), BF),
+            low,
+            low,
+            low,
+            low,
+            shape((rows, 3 * width // 2), BF),
+            low,
+            low,
+            shape((8, width), F32),
         ),
-        in_specs=[any_spec] * 8,
-        out_specs=(any_spec,) * 6,
+        in_specs=[pl.BlockSpec(memory_space=pltpu.SMEM)] + [any_spec] * 15 + [vmem_spec] * 3,
+        out_specs=(any_spec,) * 10,
         scratch_shapes=[
             pltpu.VMEM((rows, width), BF),
             pltpu.VMEM((rows, width), BF),
-            pltpu.VMEM(gate_w.shape, BF),
-            pltpu.VMEM(up_w.shape, BF),
+            pltpu.VMEM((width, 2 * hidden), BF),
             pltpu.VMEM(down_w.shape, BF),
             pltpu.VMEM((2, rows, TILE_COLS), BF),
-            pltpu.VMEM((2, BLOCK, hidden), BF),
-            pltpu.VMEM((2, BLOCK, hidden), BF),
-            pltpu.VMEM((2, BLOCK, 2 * hidden), BF),
             pltpu.VMEM((2, BLOCK, width), BF),
-            pltpu.VMEM((2, BLOCK, hidden), BF),
-            pltpu.VMEM((SLOTS, TILE_ROWS, TILE_COLS), BF),
-            pltpu.VMEM((SLOTS, TILE_ROWS, TILE_COLS), BF),
-            pltpu.VMEM((SLOTS, TILE_ROWS // 2, TILE_COLS), BF),
-            pltpu.VMEM((SLOTS, TILE_ROWS // 4, TILE_COLS), BF),
-            pltpu.VMEM((SLOTS, TILE_ROWS // 8, TILE_COLS), BF),
-            pltpu.VMEM((SLOTS, TILE_ROWS // 16, TILE_COLS), BF),
+            pltpu.VMEM((8, width), F32),
+            pltpu.VMEM((4, 8, width), F32),
+            pltpu.VMEM((16, width), F32),
+            *ring,
             dma((5,)),
             dma((2,)),
-            dma((2, 2)),
+            dma((2, 4)),
             dma((2,)),
             dma((2,)),
             dma((2,)),
-            dma((2,)),
+            dma((3,)),
+            dma,
+            dma((4,)),
+            dma((4,)),
+            dma((2 * blocks,)),
             dma((2 * blocks,)),
             dma((SLOTS, 8)),
             dma((SLOTS, 8)),
@@ -463,7 +803,10 @@
         compiler_params=pltpu.CompilerParams(
             collective_id=1, has_side_effects=True, vmem_limit_bytes=VMEM_BYTES
         ),
-    )(hid, slope, silu, h2, dy, gate_w, up_w, down_w)
+    )(
+        lengths, hid, slope, silu, h2, dy, gate_w, up_w, down_w, resid, x, keep, z, h1, in_full, out_full,
+        gain1.reshape(1, width), gain2.reshape(1, width), taps,
+    )
 
 
 def fetch_other(weight, core, count):
@@ -506,87 +849,33 @@
 
     in_full = ordered(in_weight, in_other, 2).reshape(width, 6 * half)
     out_full = ordered(out_weight, out_other, 0)
-    taps = ordered(conv_weight, taps_other, 1).astype(F32)
+    taps = ordered(conv_weight, taps_other, 1)
     full = 2 * half
 
-    dist = distances(lengths[0], rows)
-    keep_one = (dist >= 1)[:, None].astype(F32)
-    keep_two = (dist >= 2)[:, None].astype(F32)
-    x = tokens.astype(F32)
-    dy = cotangent.astype(F32)
-    g1 = mixer_gain.astype(F32)
-    g2 = ffn_gain.astype(F32)
-    scale1 = rms_scale(x)
-    normed1 = x * scale1
-    h1b = (normed1 * g1).astype(BF)
-    proj = dot(h1b, in_full, 1, 0)
-    b_part, c_part, x_part = (proj[:, :full], proj[:, full : 2 * full], proj[:, 2 * full :])
-    mixed = b_part * x_part
-    mixed_one = shift_down(mixed, 1, keep_one)
-    mixed_two = shift_down(mixed, 2, keep_two)
-    conv_out = taps[0] * mixed + taps[1] * mixed_one + taps[2] * mixed_two
-    zb = (c_part * conv_out).astype(BF)
-    resid = x + dot(zb, out_full, 1, 0)
-    scale2 = rms_scale(resid)
-    normed2 = resid * scale2
-    h2b = (normed2 * g2).astype(BF)
-
+    h1b, keep, zb, resid, h2b = mixer_forward(
+        lengths, tokens, mixer_gain, in_full, taps, out_full, ffn_gain
+    )
     hidb, slope, silu = swiglu(h2b, gate_weight, up_weight)
-    sums, _, dh2_own, dh2_got, ffn_own, ffn_got = ffn_backward(
-        hidb, slope, silu, h2b, cotangent, gate_weight, up_weight, down_weight
+    sums, _, _, _, _, _, _, input_grad, output, small = block_backward(
+        lengths, hidb, slope, silu, h2b, cotangent, gate_weight, up_weight, down_weight, resid, tokens,
+        keep, zb, h1b, in_full, out_full, mixer_gain, ffn_gain, taps,
     )
     hidden = gate_weight.shape[1]
-    down_sum = sums[:, :hidden].T
-    gate_sum = sums[:, hidden : 2 * hidden]
-    up_sum = sums[:, 2 * hidden :]
-
-    dh2 = dh2_own.astype(F32) + dh2_got.astype(F32)
-    d_resid, g2_grad = norm_back(dh2, normed2, scale2, g2)
-    dr1 = dy + d_resid
-    dr1b = dr1.astype(BF)
-    own = lambda v, axis: lax.dynamic_slice_in_dim(v, side * half, half, axis)
-    out_grad = dot(own(zb, 1), dr1b, 0, 0).astype(BF)
-    d_z = dot(dr1b, out_full, 1, 1)
-    d_c = d_z * conv_out
-    d_conv = d_z * c_part
-    d_own = own(d_conv, 1)
-    conv_grad = jnp.stack(
-        [
-            jnp.sum(d_own * own(mixed, 1), axis=0),
-            jnp.sum(d_own * own(mixed_one, 1), axis=0),
-            jnp.sum(d_own * own(mixed_two, 1), axis=0),
-        ],
-        0,
-    )
-    d_mixed = (
-        taps[0] * d_conv
-        + taps[1] * shift_up(d_conv * keep_one, 1)
-        + taps[2] * shift_up(d_conv * keep_two, 2)
-    )
-    d_b = (d_mixed * x_part).astype(BF)
-    d_c = d_c.astype(BF)
-    d_x = (d_mixed * b_part).astype(BF)
-    in_grad = jnp.stack(
-        [dot(h1b, own(d_b, 1), 0, 0), dot(h1b, own(d_c, 1), 0, 0), dot(h1b, own(d_x, 1), 0, 0)], 1
-    ).astype(BF)
-    d_proj = jnp.concatenate([d_b, d_c, d_x], 1)
-    dh1 = dot(d_proj, in_full, 1, 1)
-    d_input, g1_grad = norm_back(dh1, normed1, scale1, g1)
-    input_grad = (dr1 + d_input).astype(BF)
-    output = (resid + (ffn_own.astype(F32) + ffn_got.astype(F32))).astype(BF)
-    in_sum, out_sum = lax.psum((in_grad, out_grad), "dp")
-    g1_sum, conv_sum, g2_sum = lax.psum((g1_grad, conv_grad, g2_grad), "dp")
+
+    def columns(first, size):
+        return sums[:, first : first + size].astype(F32)
+
     return (
         output,
         input_grad,
-        g1_sum,
-        in_sum.astype(F32),
-        conv_sum,
-        out_sum.astype(F32),
-        g2_sum,
-        gate_sum.astype(F32),
-        up_sum.astype(F32),
-        down_sum.astype(F32),
+        small[0],
+        columns(3 * hidden + half, 3 * half).reshape(width, 3, half),
+        lax.dynamic_slice_in_dim(small[2:5], side * half, half, 1),
+        columns(3 * hidden, half).T,
+        small[1],
+        columns(hidden, hidden),
+        columns(2 * hidden, hidden),
+        columns(0, hidden).T,
     )
 
 

time: 703 us -> 500 us (0.71)
  other arithmetic: 151 us -> 31.7 us
  matrix products: 81.8 us -> 0 us
  blocking collectives: 60.9 us -> 0 us
  Pallas kernels: 308 us -> 358 us
  local copies, waits for them, and re-layouts: 23 us -> 49.6 us
  between operations: 14.8 us -> 1.21 us
    convert_element_type x11 -> x0, other arithmetic: 87 us -> none  [the longest x1 28.1 us: pair_body(): zb = (c_part * conv_out).astype(BF)]
    dot_general x8 -> x0, matrix products: 81.8 us -> none  [dot(): lax.dot_general(a, b, (((ca,), (cb,)), ((), ())), preferred_element_type=...]
    psum x1 -> x0, blocking collectives: 60.9 us -> none  [pair_body(): g1_sum, conv_sum, g2_sum = lax.psum((g1_grad, conv_grad, g2_grad), 'dp')]
    pallas_call x1 -> x2, Pallas kernels: 279 us -> 329 us  [the longest x1 302 us: block_backward(): pl.pallas_call(back_kernel, out_shape=(shape((TILE_ROWS, count * TILE_COL...]
    mul x3 -> x0, other arithmetic: 20.5 us -> none  [the longest x1 12 us: pair_body(): mixed = b_part * x_part]
    reduce_sum x3 -> x0, other arithmetic: 18.3 us -> none  [the longest x1 7.83 us: pair_body(): jnp.sum(d_own * own(mixed, 1), axis=0)]
    reshape x0 -> x4, local copies, waits for them, and re-layouts: none -> 16.4 us  [the longest x1 8.64 us: pair_body(): in_full = ordered(in_weight, in_other, 2).reshape(width, 6 * half)]
    transpose x0 -> x2, other arithmetic: none -> 14.8 us  [the longest x1 13.3 us: pair_body(): columns(0, hidden)]
  transfers between devices with their start and end apart: 6 -> 5, of which waited for: 4 -> 3; matrix products, arithmetic and copies ran while one was open for 7% -> 2% of each run, Pallas kernels for 0% -> 0%
where the time goes in v3:
time: 500 us; the launch traced here: 491 us
  Pallas kernels  358 us (72%)
  local copies, waits for them, and re-layouts  49.6 us (10%)
  waiting for transfers between devices  45.4 us (9%)
  other arithmetic  31.7 us (6%)
    pallas_call x1, Pallas kernels, block_backward(): pl.pallas_call(back_kernel, out_shape=(shape((TILE_ROWS, count * TILE_COL...  302 us
    ppermute x3, waiting for transfers between devices, swap_tensor(): return lax.ppermute(value, 'tensor', [(0, 1), (1, 0)])  45.4 us
    pallas_call x1, Pallas kernels, swiglu(): pl.pallas_call(swiglu_kernel, grid=(rows // BLOCK,), out_shape=(out, out,...  29.1 us
    unnamed x14, local copies, waits for them, and re-layouts  28 us
    pallas_call x1, Pallas kernels, mixer_forward(): pl.pallas_call(mixer_kernel, grid=(rows // BLOCK,), out_shape=(low, jax.S...  27.3 us
    transpose x1, other arithmetic, pair_body(): columns(0, hidden)  13.3 us
  transfers between devices with their start and end apart: 5, of which 3 were waited for; matrix products, arithmetic and copies ran while one was open for 2% of the time, Pallas kernels for 0%

profile of v3, /device:TPU:0, one launch (start us, length us, event | category | flops | bytes accessed | tf_op | source)
XLA Modules:
  0.0 490.8 jit_solution(8143962878258265681)
XLA Ops:
  0.7 0.0 copy-start.1
  0.7 0.0 copy-start.2
  0.7 0.0 copy-start.3
  0.7 3.2 copy.26
  3.9 1.3 constant_dynamic-slice_fusion.2
  5.2 2.9 collective-permute-start
  8.2 1.1 constant_dynamic-slice_fusion.1
  9.2 0.1 collective-permute-start.3
  9.3 34.4 %collective-permute-done = bf16[512,1536]{0,1:T(8,128)(2,1)} collective-permute-done((bf16[512,1536]{0,1:T(8,128)(2,1)}, bf16[512,1536]{0,1:T(8,128)(2,1)}, u32[]{:S(2)}, u32[]{:S(2)}) %collective-permute-start) | collective-permute-done | bytes 1572896 | tf_op jit(solution)/shard_map/ppermute | solution.py:50
  43.7 0.0 collective-permute-start.1
  43.7 10.4 %collective-permute-done.3 = bf16[256,1024]{1,0:T(8,128)(2,1)} collective-permute-done((bf16[256,1024]{1,0:T(8,128)(2,1)S(1)}, bf16[256,1024]{1,0:T(8,128)(2,1)}, u32[]{:S(2)}, u32[]{:S(2)}) %collective-permute-start.3) | collective-permute-done | bytes 524320 | tf_op jit(solution)/shard_map/ppermute | solution.py:50
  54.1 0.0 collective-permute-start.4
  54.1 0.0 copy-done.1
  54.1 1.7 collective-permute-start.2
  55.8 0.0 copy-done.2
  55.9 0.6 reshape.43.gain1_ref
  56.4 0.0 copy-done.3
  56.5 0.6 reshape.47.gain2_ref
  57.0 0.7 collective-permute-done.2
  57.7 0.6 pad_maximum_fusion.4.taps_ref
  58.3 0.0 collective-permute-done.4
  58.3 1.3 broadcast_select_fusion.7
  59.6 1.8 broadcast_select_fusion.5
  61.4 1.5 pad_maximum_fusion.2.out_ref
  62.9 0.0 collective-permute-done.1
  62.9 2.1 broadcast_select_fusion.3
  65.0 0.4 pad_maximum_fusion.1
  65.4 0.4 broadcast_select_fusion.1
  65.8 3.4 pad_maximum_fusion
  69.2 8.6 %copy.28.in_ref = bf16[1024,3072]{1,0:T(8,128)(2,1)} copy(bf16[1024,3072]{0,1:T(8,128)(2,1)} %bitcast.10) | data formatting | bytes 12582912 | tf_op jit(solution)/shard_map/reshape | solution.py:850
  77.9 27.3 %shard_map.186 = (bf16[2048,1024]{1,0:T(8,128)(2,1)}, bf16[2048,4096]{1,0:T(8,128)(2,1)}, bf16[2048,1024]{1,0:T(8,128)(2,1)}, f32[2048,1024]{1,0:T(8,128)}, bf16[2048,1024]{1,0:T(8,128)(2,1)}) custom-call(s32[1,3]{1,0:T(1,128)} %lengths_ref.3, bf16[2048,1024]{1,0:T(8,128)(2,1)} %x_ref.3, bf16[1,1024]{1,0:T(2,128)(2,1)} %reshape.43.gain1_ref, ...), custom_call_target="tpu_custom_call" | custom-call | tf_op jit(solution)/shard_map/pallas_call | solution.py:124
  105.1 29.1 %shard_map.187 = (bf16[2048,2304]{1,0:T(8,128)(2,1)}, bf16[2048,2304]{1,0:T(8,128)(2,1)}, bf16[2048,2304]{1,0:T(8,128)(2,1)}) custom-call(bf16[2048,1024]{1,0:T(8,128)(2,1)} %get-tuple-element.22.h2_ref, bf16[1024,2304]{1,0:T(8,128)(2,1)} %gate_ref.3, bf16[1024,2304]{1,0:T(8,128)(2,1)} %up_ref.3), custom_call_target="tpu_custom_call" | custom-call | tf_op jit(solution)/shard_map/pallas_call | solution.py:166
  134.2 301.8 %shard_map.188 = (bf16[1024,8960]{1,0:T(8,128)(2,1)}, bf16[2048,4608]{1,0:T(8,128)(2,1)}, bf16[2048,1024]{1,0:T(8,128)(2,1)}, bf16[2048,1024]{1,0:T(8,128)(2,1)}...) custom-call(s32[1,3]{1,0:T(1,128)} %lengths_ref.3, ...), custom_call_target="tpu_custom_call" | custom-call | tf_op jit(solution)/shard_map/pallas_call | solution.py:760
  436.0 1.4 fusion
  437.4 0.8 slice.26
  438.2 1.5 convert_bitcast_fusion.1
  439.7 5.5 %slice_convert_fusion.2 = f32[1024,1536]{1,0:T(8,128)} fusion(bf16[1024,8960]{1,0:T(8,128)(2,1)} %get-tuple-element.33), kind=kLoop, calls=%fused_computation.5 | loop fusion | flops 1572864 | bytes 9437184 | tf_op jit(solution)/shard_map/reshape | solution.py:872
  445.2 13.3 %convert_bitcast_fusion = (f32[2304,1024]{0,1:T(8,128)}, f32[1024,2304]{1,0:T(8,128)}, f32[1024,2304]{1,0:T(8,128)}) fusion(bf16[1024,8960]{1,0:T(8,128)(2,1)} %get-tuple-element.33), kind=kLoop, calls=%fused_computation | loop fusion | flops 7077888 | bytes 42467328 | tf_op jit(solution)/shard_map/transpose | solution.py:878
  458.4 1.8 copy.32
  460.2 6.6 %copy.30 = f32[1024,1536]{0,1:T(8,128)} copy(f32[1024,1536]{1,0:T(8,128)} %slice_convert_fusion.2) | data formatting | bytes 12582912 | tf_op jit(solution)/shard_map/reshape | solution.py:872
  466.8 6.6 %copy.31 = f32[1024,3,512]{2,0,1:T(8,128)} copy(f32[1024,3,512]{0,2,1:T(8,128)} %bitcast.11) | data formatting | bytes 12582912
  473.4 9.6 %copy.33 = f32[2304,1024]{1,0:T(8,128)} copy(f32[2304,1024]{0,1:T(8,128)} %get-tuple-element.54) | data formatting | bytes 18874368
  482.9 0.6 constant_dynamic-slice_fusion
  483.5 0.0 copy-start
  483.5 4.8 copy.36
  488.3 0.0 copy-done
  488.4 2.0 copy.37
  (1 shorter events, 0.0 us)
Async XLA Ops:
  0.7 53.4 %copy-start.1 = (bf16[3,512]{1,0:T(4,128)(2,1)S(1)}, bf16[3,512]{1,0:T(4,128)(2,1)}, u32[]{:S(2)}) copy-start(bf16[3,512]{1,0:T(4,128)(2,1)} %param.16) | copy-start | bytes 9220
  0.7 55.2 %copy-start.2 = (bf16[1024]{0:T(1024)(128)(2,1)S(1)}, bf16[1024]{0:T(1024)(128)(2,1)}, u32[]{:S(2)}) copy-start(bf16[1024]{0:T(1024)(128)(2,1)} %param.14) | copy-start | bytes 6148
  0.7 55.8 %copy-start.3 = (bf16[1024]{0:T(1024)(128)(2,1)S(1)}, bf16[1024]{0:T(1024)(128)(2,1)}, u32[]{:S(2)}) copy-start(bf16[1024]{0:T(1024)(128)(2,1)} %param.18) | copy-start | bytes 6148
  5.2 38.5 %collective-permute-start = (bf16[512,1536]{0,1:T(8,128)(2,1)}, bf16[512,1536]{0,1:T(8,128)(2,1)}, u32[]{:S(2)}, u32[]{:S(2)}) collective-permute-start(bf16[512,1536]{0,1:T(8,128)(2,1)} %constant_dynamic-slice_fusion.2), channel_id=1, source_target_pairs={{0,1},{1,0},{2,3},{3,2},{4,5},{5,4},{6,7},{7,6},{8,9},{9,8},{10,11... | collective-permute-start | bytes 4718600 | tf_op jit(solution)/shard_map/ppermute | solution.py:50
  9.2 44.9 %collective-permute-start.3 = (bf16[256,1024]{1,0:T(8,128)(2,1)S(1)}, bf16[256,1024]{1,0:T(8,128)(2,1)}, u32[]{:S(2)}, u32[]{:S(2)}) collective-permute-start(bf16[256,1024]{1,0:T(8,128)(2,1)S(1)} %constant_dynamic-slice_fusion.1), channel_id=1, source_target_pairs={{0,1},{1,0},{2,3},{3,2},{4,5},{5,4},{6,7},{7,6},{8,9},{9,8},{10,11... | collective-permute-start | bytes 1572872 | tf_op jit(solution)/shard_map/ppermute | solution.py:50
  43.7 19.2 %collective-permute-start.1 = (bf16[512,1536]{0,1:T(8,128)(2,1)}, bf16[512,1536]{0,1:T(8,128)(2,1)}, u32[]{:S(2)}, u32[]{:S(2)}) collective-permute-start(bf16[512,1536]{0,1:T(8,128)(2,1)} %collective-permute-done), channel_id=1, source_target_pairs={{0,2},{2,0},{4,6},{6,4},{8,10},{10,8},{12,14},{14,12},{16,18},{18,... | collective-permute-start | bytes 4718600 | tf_op jit(solution)/shard_map/ppermute | solution.py:54
  54.1 4.2 collective-permute-start.4
  54.1 3.6 collective-permute-start.2
  483.5 4.8 copy-start
